TPU v7x, 128 devices: a whole 4x4x4 slice. The times are simulated.
128 devices in a mesh: gx: 8 (over x, core), gy: 16 (over z, y).
Axes of the slice: x: 4, y: 4, z: 4, core: 2. Of those that a mesh axis runs over, the one named last changes fastest.
Arguments:
- latents: bfloat16 [8, 16, 24, 512, 128], P('gx', 'gy'), may hold values from -6 to 6
- gain_first: float32 [128], replicated, may hold values from 0.5 to 1.5
- conv_first: bfloat16 [7, 128, 128], replicated, may hold values from -0.1875 to 0.1875
- gain_second: float32 [128], replicated, may hold values from 0.5 to 1.5
- conv_second: bfloat16 [7, 128, 128], replicated, may hold values from -0.1875 to 0.1875
- upward: bfloat16 [2, 2, 2, 128, 128], replicated, may hold values from -0.5 to 0.5
- neighbour_owner: int32 [8, 16, 24, 6], P('gx', 'gy'), may hold values from -1 to 127, as said below
- neighbour_slot: int32 [8, 16, 24, 6], P('gx', 'gy'), may hold values from -1 to 23, as said below
- destination_device: int32 [8, 16, 24], P('gx', 'gy'), may hold values from -1 to 15, as said below
- destination_slot: int32 [8, 16, 24], P('gx', 'gy'), may hold values from -1 to 23, as said below
Outputs:
- children: bfloat16 [8, 16, 192, 512, 128], P('gx', 'gy')
Inputs may be any that keep to these rules, and one draw needn't show every extreme that they name: `neighbour_owner`: -1 where the slot is empty or the face has no active neighbour. Across an x face the owner is this device or the adjacent device along gx on that side, across a y face this device or the adjacent device along gy on that side, across a z face this device; faces on the grid's outer boundary have no neighbour. Neighbourhood is symmetric and agrees with neighbour_slot. `neighbour_slot`: -1 exactly where neighbour_owner is -1; else an occupied slot of the owner. `destination_device`: -1 for empty slots; the occupied slots of a device are its first ones. In each gx group the occupied blocks, taken in order of gy index and slot, go to the group's devices in turn from some starting device, so at most 2 blocks go from one device to one destination. `destination_slot`: -1 for empty slots; for the r-th occupied block of a gx group (counted from 0) it is r // 16; occupied blocks of a group have distinct destinations and slots.
All inputs are finite; a program needn't handle non-finite values.
Results may differ from a plain program's by a relative error of at most 0.0054.
Values may be sent and summed in bfloat16 or wider, within the bound.
A program may use at most 256 MiB of HBM per device.

v0:
```python
import jax
import jax.numpy as jnp
from jax import lax
from jax.sharding import PartitionSpec as P

E = 8


def shifted_2(block, axis, distance):
    devices = range(lax.axis_size(axis))
    route = [(i - distance, i) for i in devices if i - distance in devices]
    return lax.ppermute(block, axis, route)


def normed(values, gain_vec):
    floats = values.astype(jnp.float32)
    scale = lax.rsqrt(jnp.mean(floats * floats, axis=-1, keepdims=True) + 1e-06)
    return jax.nn.silu(floats * scale * gain_vec).astype(jnp.bfloat16)


def taps(active, face_list, kernel):
    count_blocks = active.shape[0]
    edge = active.shape[1]
    channels = active.shape[-1]
    stacked = kernel.transpose(1, 0, 2).reshape(channels, 7 * channels)
    whole = jnp.dot(active.reshape(-1, channels), stacked, preferred_element_type=jnp.float32)
    whole = whole.reshape(count_blocks, edge, edge, edge, 7 * channels)
    summed = whole[..., :channels]
    for face_index in range(6):
        tap_index = face_index + 1
        part = whole[..., tap_index * channels : (tap_index + 1) * channels]
        face_term = jnp.dot(
            face_list[face_index].reshape(-1, channels),
            kernel[tap_index],
            preferred_element_type=jnp.float32,
        )
        face_term = face_term.reshape(face_list[face_index].shape)
        axis = 1 + face_index // 2
        face_term = jnp.expand_dims(face_term, axis)
        if face_index % 2 == 0:
            inner = lax.slice_in_dim(part, 1, edge, axis=axis)
            shifted = jnp.concatenate([inner, face_term], axis=axis)
        else:
            inner = lax.slice_in_dim(part, 0, edge - 1, axis=axis)
            shifted = jnp.concatenate([face_term, inner], axis=axis)
        summed = summed + shifted
    return summed.reshape(-1, channels)


def subdivide(blocks, upward):
    count_blocks = blocks.shape[0]
    channels = blocks.shape[-1]
    half = E // 2
    upward_mat = upward.transpose(3, 0, 1, 2, 4).reshape(channels, 8 * channels)
    product = jnp.dot(
        blocks.reshape(-1, channels), upward_mat, preferred_element_type=jnp.float32
    ).astype(jnp.bfloat16)
    product = product.reshape(count_blocks, 2, half, 2, half, 2, half, 2, 2, 2, channels)
    product = product.transpose(0, 1, 3, 5, 2, 7, 4, 8, 6, 9, 10)
    return product.reshape(count_blocks, 8, E**3, channels)


def choose(local_layers, remote_layers, owner_col, slot_col, own_index):
    number = local_layers.shape[0]
    if remote_layers is None:
        candidates = local_layers
        offset = slot_col
    else:
        candidates = jnp.concatenate([local_layers, remote_layers], axis=0)
        offset = slot_col + jnp.where(owner_col == own_index, 0, number)
    picked = jnp.take(candidates, jnp.clip(offset, 0, candidates.shape[0] - 1), axis=0)
    return jnp.where((slot_col >= 0)[:, None, None, None], picked, jnp.zeros_like(picked))


def convolve(active, owners, slot_ids, own_index, kernel):
    low_x = active[:, 0]
    high_x = active[:, -1]
    low_y = active[:, :, 0]
    high_y = active[:, :, -1]
    from_east = shifted_2(low_x, "gx", -1)
    from_west = shifted_2(high_x, "gx", 1)
    from_north = shifted_2(low_y, "gy", -1)
    from_south = shifted_2(high_y, "gy", 1)
    face_list = [
        choose(low_x, from_east, owners[:, 0], slot_ids[:, 0], own_index),
        choose(high_x, from_west, owners[:, 1], slot_ids[:, 1], own_index),
        choose(low_y, from_north, owners[:, 2], slot_ids[:, 2], own_index),
        choose(high_y, from_south, owners[:, 3], slot_ids[:, 3], own_index),
        choose(active[:, :, :, 0], None, owners[:, 4], slot_ids[:, 4], own_index),
        choose(active[:, :, :, -1], None, owners[:, 5], slot_ids[:, 5], own_index),
    ]
    return taps(active, face_list, kernel)


def per_device(
    latents,
    gain_first,
    conv_first,
    gain_second,
    conv_second,
    upward,
    neighbour_owner,
    neighbour_slot,
    destination_device,
    destination_slot,
):
    number = latents.shape[2]
    channels = latents.shape[-1]
    blocks = latents.reshape(number, E, E, E, channels)
    owners = neighbour_owner.reshape(number, 6)
    slot_ids = neighbour_slot.reshape(number, 6)
    own_index = lax.axis_index("gx") * lax.axis_size("gy") + lax.axis_index("gy")
    first = normed(blocks, gain_first)
    mixed = convolve(first, owners, slot_ids, own_index, conv_first)
    second = normed(mixed.reshape(number, E, E, E, channels), gain_second)
    branch = convolve(second, owners, slot_ids, own_index, conv_second)
    hidden = (blocks.reshape(-1, channels).astype(jnp.float32) + branch).astype(jnp.bfloat16)
    hidden = hidden.reshape(number, E**3, channels)
    dest_dev = destination_device.reshape(number)
    dest_slot = destination_slot.reshape(number)
    peer_count = lax.axis_size("gy")
    capacity = (number + peer_count - 1) // peer_count
    slot_range = jnp.arange(number, dtype=jnp.int32)
    earlier = (slot_range[None, :] < slot_range[:, None]) & (dest_dev[None, :] == dest_dev[:, None])
    rank_in = jnp.sum(earlier.astype(jnp.int32), axis=1)
    peer_range = jnp.arange(peer_count, dtype=jnp.int32)
    capacity_range = jnp.arange(capacity, dtype=jnp.int32)
    matches = (dest_dev[None, None, :] == peer_range[:, None, None]) & (
        rank_in[None, None, :] == capacity_range[None, :, None]
    )
    matches_int = matches.astype(jnp.int32)
    source = jnp.sum(matches_int * slot_range, axis=-1)
    present = jnp.any(matches, axis=-1)
    send_slot = jnp.where(present, jnp.sum(matches_int * dest_slot, axis=-1), -1)
    payload = jnp.take(hidden, source.reshape(-1), axis=0).reshape(
        peer_count, capacity, E**3, channels
    )
    arrived, arrived_slot = (
        lax.all_to_all(payload, "gy", split_axis=0, concat_axis=0, tiled=True),
        lax.all_to_all(send_slot, "gy", split_axis=0, concat_axis=0, tiled=True),
    )
    arrived_flat = arrived.reshape(peer_count * capacity, E**3, channels)
    arrived_ids = arrived_slot.reshape(-1)
    hits = arrived_ids[None, :] == slot_range[:, None]
    anchor = jnp.sum(
        hits.astype(jnp.int32) * jnp.arange(peer_count * capacity, dtype=jnp.int32)[None, :], axis=1
    )
    filled = jnp.any(hits, axis=1)
    picked = jnp.take(arrived_flat, anchor, axis=0)
    moved = jnp.where(filled[:, None, None], picked, jnp.zeros_like(picked))
    children = subdivide(moved, upward)
    return children.reshape(1, 1, number * 8, E**3, channels)


def solution(mesh):
    placed = (
        P("gx", "gy", None, None, None),
        P(),
        P(),
        P(),
        P(),
        P(),
        P("gx", "gy", None, None),
        P("gx", "gy", None, None),
        P("gx", "gy", None),
        P("gx", "gy", None),
    )
    return jax.shard_map(
        per_device,
        mesh=mesh,
        in_specs=placed,
        out_specs=P("gx", "gy", None, None, None),
        check_vma=False,
    )
```

profile of v0, /device:TPU:1, one launch (start us, length us, event | category | flops | bytes accessed | tf_op | source)
XLA Modules:
  0.0 449.4 jit_solution(11830204580467772886)
XLA Ops:
  0.0 3.7 multiply_reduce_fusion.1
  3.9 1.5 copy.36
  5.4 4.4 multiply_convert_fusion.1
  11.1 4.8 %collective-permute-start.3 = (bf16[24,8,8,128]{3,2,1,0:T(8,128)(2,1)}, bf16[24,8,8,128]{3,2,1,0:T(8,128)(2,1)}, u32[]{:S(2)}, u32[]{:S(2)}) collective-permute-start(bf16[24,8,8,128]{3,2,1,0:T(8,128)(2,1)} %get-tuple-element.44), channel_id=1, source_target_pairs={{0,1},{1,2},{2,3},{3,4},{4,5},{5,6},{6,7},{7,8},{8,9},{9,10},{10,1... | collective-permute-start | bytes 1179656 | tf_op jit(solution)/shard_map/ppermute | solution.py:12
  18.2 3.9 collective-permute-start.1
  22.1 1.9 collective-permute-start
  25.2 9.1 %all-to-all-start = ((s32[16,1,2]{2,1,0:T(1,128)}), s32[16,1,2]{2,1,0:T(1,128)S(1)}, u32[]{:S(2)}, u32[]{:S(2)}) async-start(s32[16,1,2]{2,1,0:T(1,128)} %copy.31), calls=%async_computation | async-start | bytes 16384 | tf_op jit(solution)/shard_map/all_to_all | solution.py:140
  34.4 5.7 %fusion.129 = (bf16[24,8,8,1,128]{4,3,2,1,0:T(2,128)(2,1)}, bf16[24,8,8,1,128]{4,3,2,1,0:T(2,128)(2,1)}) fusion(bf16[24,8,8,8,128]{4,3,2,1,0:T(8,128)(2,1)} %copy-done.3), kind=kLoop, calls=%fused_computation.243 | loop fusion | bytes 1572864 | tf_op jit(solution)/shard_map/slice | solution.py:89
  40.1 3.4 multiply_convert_fusion.2
  44.6 18.4 %fusion.130 = f32[24,8,8,8,896]{4,3,2,1,0:T(8,128)} fusion(bf16[24,8,8,8,128]{4,3,2,1,0:T(8,128)(2,1)} %bitcast.212, bf16[128,896,1,1,1]{0,1,4,3,2:T(8,128)(2,1)S(1)} %bitcast.224), kind=kOutput, calls=%fused_computation.244 | convolution fusion | flops 2818572288 | bytes 47415296 | tf_op jit(solution)/shard_map/dot_general | solution.py:26
  63.0 12.4 %fusion.127 = (f32[24,8,8,7,128]{4,3,2,1,0:T(8,128)}, f32[24,8,8,7,128]{4,3,2,1,0:T(8,128)}) fusion(f32[24,8,8,8,896]{4,3,2,1,0:T(8,128)} %fusion.130), kind=kLoop, calls=%fused_computation.241 | loop fusion | bytes 22020096 | tf_op jit(solution)/shard_map/slice | solution.py:41
  75.4 10.6 %fusion.125 = (f32[24,7,8,8,128]{4,3,2,1,0:T(8,128)}, f32[24,7,8,8,128]{4,3,2,1,0:T(8,128)}) fusion(f32[24,8,8,8,896]{4,3,2,1,0:T(8,128)} %fusion.130), kind=kLoop, calls=%fused_computation.239 | loop fusion | bytes 22020096 | tf_op jit(solution)/shard_map/slice | solution.py:41
  86.1 9.6 %fusion.126 = (f32[24,8,7,8,128]{4,3,2,1,0:T(8,128)}, f32[24,8,7,8,128]{4,3,2,1,0:T(8,128)}) fusion(f32[24,8,8,8,896]{4,3,2,1,0:T(8,128)} %fusion.130), kind=kLoop, calls=%fused_computation.240 | loop fusion | bytes 22020096 | tf_op jit(solution)/shard_map/slice | solution.py:41
  98.9 2.3 copy_bitcast_fusion.2
  101.2 2.3 gather_fusion.6
  103.5 1.4 gather_fusion.7
  104.9 2.3 fusion.14
  107.1 2.2 fusion.13
  112.5 1.8 copy.37
  116.3 2.1 pad_maximum_fusion.3
  118.4 1.9 gather_fusion.5
  120.3 2.1 pad_maximum_fusion.2
  122.3 2.6 gather_fusion.4
  125.0 2.1 pad_maximum_fusion.1
  127.0 2.6 gather_fusion.3
  129.7 2.1 pad_maximum_fusion
  131.7 2.5 gather_fusion.2
  139.3 15.0 %multiply_reduce_fusion = (f32[24,8,8,8]{3,2,1,0:T(8,128)S(1)}, f32[24,8,8,8,128]{4,3,2,1,0:T(8,128)S(1)}) fusion(f32[24,8,8,7,128]{4,3,2,1,0:T(8,128)} %get-tuple-element.34, f32[24,8,8,1,128]{4,3,2,1,0:T(1,128)} %bitcast.217, f32[24,8,8,1,128]{4,3,2,1,0:T(1,128)} %bitcast.216, f32[24,8,8,7,128]{4,3,2,1,0:T(8,128)} %get-tuple-element.33, ...), kind=kLoop, calls=%fused_computation.30 | loop fusion | flops 22007808 | bytes 50380800 | tf_op jit(solution)/shard_map/reduce_sum | solution.py:17
  154.5 2.0 multiply_convert_fusion
  159.2 18.4 %fusion.131 = f32[24,8,8,8,896]{4,3,2,1,0:T(8,128)} fusion(bf16[24,8,8,8,128]{4,3,2,1,0:T(8,128)(2,1)} %copy-done.1, bf16[128,896,1,1,1]{0,1,4,3,2:T(8,128)(2,1)S(1)} %bitcast.223), kind=kOutput, calls=%fused_computation.245 | convolution fusion | flops 2818572288 | bytes 47415296 | tf_op jit(solution)/shard_map/dot_general | solution.py:26
  177.7 12.3 %fusion.122 = (f32[24,8,8,7,128]{4,3,2,1,0:T(8,128)}, f32[24,8,8,7,128]{4,3,2,1,0:T(8,128)}) fusion(f32[24,8,8,8,896]{4,3,2,1,0:T(8,128)} %fusion.131), kind=kLoop, calls=%fused_computation.236 | loop fusion | bytes 22020096 | tf_op jit(solution)/shard_map/slice | solution.py:44
  189.9 9.6 %fusion.123 = (f32[24,8,7,8,128]{4,3,2,1,0:T(8,128)}, f32[24,8,7,8,128]{4,3,2,1,0:T(8,128)}) fusion(f32[24,8,8,8,896]{4,3,2,1,0:T(8,128)} %fusion.131), kind=kLoop, calls=%fused_computation.237 | loop fusion | bytes 22020096 | tf_op jit(solution)/shard_map/slice | solution.py:44
  199.5 10.8 %fusion.124 = (f32[24,7,8,8,128]{4,3,2,1,0:T(8,128)}, f32[24,7,8,8,128]{4,3,2,1,0:T(8,128)}) fusion(f32[24,8,8,8,896]{4,3,2,1,0:T(8,128)} %fusion.131), kind=kLoop, calls=%fused_computation.238 | loop fusion | bytes 22020096 | tf_op jit(solution)/shard_map/slice | solution.py:44
  210.4 2.6 fusion.128
  213.0 4.1 collective-permute-start.7
  218.4 4.5 %collective-permute-start.5 = (bf16[24,8,8,128]{3,2,1,0:T(8,128)(2,1)}, bf16[24,8,8,128]{3,2,1,0:T(8,128)(2,1)}, u32[]{:S(2)}, u32[]{:S(2)}) collective-permute-start(bf16[24,8,8,128]{3,2,1,0:T(8,128)(2,1)} %get-tuple-element.39), channel_id=1, source_target_pairs={{0,16},{16,32},{32,48},{48,64},{64,80},{80,96},{96,112},{1,17},{17... | collective-permute-start | bytes 1179656 | tf_op jit(solution)/shard_map/ppermute | solution.py:12
  222.9 2.1 collective-permute-start.4
  225.8 2.5 gather_fusion.12
  228.3 2.3 fusion.12
  230.6 1.9 copy.70
  232.5 2.5 gather_fusion.13
  235.0 2.2 fusion.11
  237.2 2.1 pad_maximum_fusion.7
  239.3 2.6 gather_fusion.11
  241.9 2.1 pad_maximum_fusion.6
  244.0 2.6 gather_fusion.10
  246.6 2.1 pad_maximum_fusion.5
  248.7 2.6 gather_fusion.9
  251.3 2.2 convolution_bitcast_fusion
  253.5 2.3 convolution_bitcast_fusion.1
  255.8 2.3 convolution_bitcast_fusion.2
  258.1 2.0 pad_maximum_fusion.4
  260.0 1.8 gather_fusion.8
  262.9 15.8 %fusion.4 = f32[24,8,8,8,128]{4,3,2,1,0:T(8,128)S(1)} fusion(f32[24,8,8,8,896]{4,3,2,1,0:T(8,128)} %fusion.131, f32[24,1,8,8,128]{4,3,2,1,0:T(8,128)S(1)} %convolution_bitcast_fusion.3, f32[24,7,8,8,128]{4,3,2,1,0:T(8,128)} %get-tuple-element.28, f32[24,7,8,8,128]{4,3,2,1,0:T(8,128)} %get-tuple-element.27, ...), kind=kLoop, calls=%fused_computation.20 | loop fusion | flops 18874368 | bytes 50331648 | tf_op jit(solution)/shard_map/add | solution.py:46
  278.7 2.6 fusion.10
  281.3 5.1 %gather_fusion = bf16[32,512,128]{2,1,0:T(8,128)(2,1)} fusion(bf16[24,512,128]{2,1,0:T(8,128)(2,1)} %fusion.10, s32[1024]{0:T(1024)} %pad_clamp_fusion.1), kind=kCustom, calls=%fused_computation.12 | custom fusion | bytes 8388736 | tf_op jit(solution)/shard_map/jit(_take)/gather | solution.py:135
  286.4 4.7 %broadcast_select_fusion = bf16[16,2,512,128]{3,2,1,0:T(8,128)(2,1)} fusion(bf16[16,2,512,128]{3,2,1,0:T(8,128)(2,1)} %bitcast.214, pred[16,2]{1,0:T(8,128)(4,1)S(1)} %copy.32), kind=kLoop, calls=%fused_computation.34 | loop fusion | flops 2097152 | bytes 8388640 | tf_op jit(solution)/shard_map/jit(_take)/select_n | solution.py:135
  291.0 7.2 %all-to-all-start.1 = ((bf16[16,2,512,128]{3,2,1,0:T(8,128)(2,1)}), bf16[16,2,512,128]{3,2,1,0:T(8,128)(2,1)}, u32[]{:S(2)}, u32[]{:S(2)}) async-start(bf16[16,2,512,128]{3,2,1,0:T(8,128)(2,1)} %broadcast_select_fusion), calls=%async_computation.1 | async-start | bytes 8388608 | tf_op jit(solution)/shard_map/all_to_all | solution.py:139
  300.0 60.1 %all-to-all-done.1 = bf16[16,2,512,128]{3,2,1,0:T(8,128)(2,1)} async-done(((bf16[16,2,512,128]{3,2,1,0:T(8,128)(2,1)}), bf16[16,2,512,128]{3,2,1,0:T(8,128)(2,1)}, u32[]{:S(2)}, u32[]{:S(2)}) %all-to-all-start.1) | async-done | bytes 4194336 | tf_op jit(solution)/shard_map/all_to_all | solution.py:139
  360.1 4.9 %gather_fusion.1 = bf16[24,512,128]{2,1,0:T(8,128)(2,1)} fusion(bf16[32,512,128]{2,1,0:T(8,128)(2,1)} %bitcast.84, s32[1024]{0:T(1024)S(1)} %pad_clamp_fusion), kind=kCustom, calls=%fused_computation.13 | custom fusion | bytes 6291552 | tf_op jit(solution)/shard_map/jit(_take)/gather | solution.py:149
  365.0 2.3 select_select_fusion
  367.3 12.4 %convolution_convert_fusion = bf16[12288,1024]{1,0:T(8,128)(2,1)} fusion(bf16[12288,128]{1,0:T(8,128)(2,1)S(1)} %bitcast.213, bf16[128,1024]{0,1:T(8,128)(2,1)S(1)} %bitcast.221), kind=kOutput, calls=%fused_computation.14 | convolution fusion | flops 3233808384 | bytes 28573696 | tf_op jit(solution)/shard_map/dot_general | solution.py:55
  379.7 40.5 %reshape.457 = bf16[24,2,4,2,4,2,4,2,2,2,128]{10,9,8,7,6,5,4,3,2,1,0:T(2,128)(2,1)} reshape(bf16[12288,1024]{1,0:T(8,128)(2,1)} %convolution_convert_fusion) | data formatting | bytes 50331648 | tf_op jit(solution)/shard_map/reshape | solution.py:58
  420.2 29.0 %copy.41 = bf16[24,2,2,2,4,2,4,2,4,2,128]{10,9,8,7,6,5,4,3,2,1,0:T(2,128)(2,1)} copy(bf16[24,2,2,2,4,2,4,2,4,2,128]{10,9,7,5,8,3,6,2,4,1,0:T(2,128)(2,1)} %bitcast.210) | data formatting | bytes 50331648 | tf_op jit(solution)/shard_map/transpose | solution.py:59
  (84 shorter events, 27.1 us)
Async XLA Ops:
  0.0 5.4 %copy-start = (bf16[1,1,24,512,128]{4,3,2,1,0:T(8,128)(2,1)S(1)}, bf16[1,1,24,512,128]{4,3,2,1,0:T(8,128)(2,1)}, u32[]{:S(2)}) copy-start(bf16[1,1,24,512,128]{4,3,2,1,0:T(8,128)(2,1)} %param.14) | copy-start | bytes 9437188
  3.7 20.3 %copy-start.12 = (s32[1,1,24]{2,1,0:T(1,128)S(1)}, s32[1,1,24]{2,1,0:T(1,128)}, u32[]{:S(2)}) copy-start(s32[1,1,24]{2,1,0:T(1,128)} %param.22) | copy-start | bytes 292
  3.8 20.6 %copy-start.13 = (s32[1,1,24]{2,1,0:T(1,128)S(1)}, s32[1,1,24]{2,1,0:T(1,128)}, u32[]{:S(2)}) copy-start(s32[1,1,24]{2,1,0:T(1,128)} %param.23) | copy-start | bytes 292
  5.4 34.7 %copy-start.10 = (f32[128]{0:T(128)S(1)}, f32[128]{0:T(128)}, u32[]{:S(2)}) copy-start(f32[128]{0:T(128)} %param.15) | copy-start | bytes 1540
  9.8 7.4 %copy-start.3 = (bf16[24,8,8,8,128]{4,3,2,1,0:T(8,128)(2,1)}, bf16[24,8,8,8,128]{4,3,2,1,0:T(8,128)(2,1)S(1)}, u32[]{:S(2)}) copy-start(bf16[24,8,8,8,128]{4,3,2,1,0:T(8,128)(2,1)S(1)} %multiply_convert_fusion.1) | copy-start | bytes 9437188
  11.1 105.2 %collective-permute-start.3 = (bf16[24,8,8,128]{3,2,1,0:T(8,128)(2,1)}, bf16[24,8,8,128]{3,2,1,0:T(8,128)(2,1)}, u32[]{:S(2)}, u32[]{:S(2)}) collective-permute-start(bf16[24,8,8,128]{3,2,1,0:T(8,128)(2,1)} %get-tuple-element.44), channel_id=1, source_target_pairs={{0,1},{1,2},{2,3},{3,4},{4,5},{5,6},{6,7},{7,8},{8,9},{9,10},{10,1... | collective-permute-start | bytes 1179656 | tf_op jit(solution)/shard_map/ppermute | solution.py:12
  15.9 104.4 %collective-permute-start.2 = (bf16[24,8,8,128]{3,2,1,0:T(8,128)(2,1)}, bf16[24,8,8,128]{3,2,1,0:T(8,128)(2,1)}, u32[]{:S(2)}, u32[]{:S(2)}) collective-permute-start(bf16[24,8,8,128]{3,2,1,0:T(8,128)(2,1)} %get-tuple-element.43), channel_id=1, source_target_pairs={{1,0},{2,1},{3,2},{4,3},{5,4},{6,5},{7,6},{8,7},{9,8},{10,9},{11,1... | collective-permute-start | bytes 1179656 | tf_op jit(solution)/shard_map/ppermute | solution.py:12
  18.2 106.8 %collective-permute-start.1 = (bf16[24,8,8,128]{3,2,1,0:T(8,128)(2,1)}, bf16[24,8,8,128]{3,2,1,0:T(8,128)(2,1)}, u32[]{:S(2)}, u32[]{:S(2)}) collective-permute-start(bf16[24,8,8,128]{3,2,1,0:T(8,128)(2,1)} %get-tuple-element.42), channel_id=1, source_target_pairs={{0,16},{16,32},{32,48},{48,64},{64,80},{80,96},{96,112},{1,17},{17... | collective-permute-start | bytes 1179656 | tf_op jit(solution)/shard_map/ppermute | solution.py:12
  22.1 107.5 %collective-permute-start = (bf16[24,8,8,128]{3,2,1,0:T(8,128)(2,1)}, bf16[24,8,8,128]{3,2,1,0:T(8,128)(2,1)}, u32[]{:S(2)}, u32[]{:S(2)}) collective-permute-start(bf16[24,8,8,128]{3,2,1,0:T(8,128)(2,1)} %get-tuple-element.41), channel_id=1, source_target_pairs={{16,0},{32,16},{48,32},{64,48},{80,64},{96,80},{112,96},{17,1},{33... | collective-permute-start | bytes 1179656 | tf_op jit(solution)/shard_map/ppermute | solution.py:12
  25.2 265.8 %all-to-all-start = ((s32[16,1,2]{2,1,0:T(1,128)}), s32[16,1,2]{2,1,0:T(1,128)S(1)}, u32[]{:S(2)}, u32[]{:S(2)}) async-start(s32[16,1,2]{2,1,0:T(1,128)} %copy.31), calls=%async_computation | async-start | bytes 16384 | tf_op jit(solution)/shard_map/all_to_all | solution.py:140
  86.1 10.3 %copy-start.8 = (s32[1,1,24,6]{2,1,3,0:T(1,128)S(1)}, s32[1,1,24,6]{2,1,3,0:T(1,128)}, u32[]{:S(2)}) copy-start(s32[1,1,24,6]{2,1,3,0:T(1,128)} %param.21) | copy-start | bytes 1732
  86.1 10.3 %copy-start.9 = (s32[1,1,24,6]{2,1,3,0:T(1,128)S(1)}, s32[1,1,24,6]{2,1,3,0:T(1,128)}, u32[]{:S(2)}) copy-start(s32[1,1,24,6]{2,1,3,0:T(1,128)} %param.20) | copy-start | bytes 1732
  98.9 13.0 %copy-start.7 = (s32[1024]{0:T(1024)}, s32[1024]{0:T(1024)S(1)}, u32[]{:S(2)}) copy-start(s32[1024]{0:T(1024)S(1)} %get-tuple-element.66) | copy-start | bytes 12292
  98.9 13.6 %copy-start.6 = (s32[1024]{0:T(1024)}, s32[1024]{0:T(1024)S(1)}, u32[]{:S(2)}) copy-start(s32[1024]{0:T(1024)S(1)} %get-tuple-element.65) | copy-start | bytes 12292
  139.3 15.2 %copy-start.11 = (f32[128]{0:T(128)S(1)}, f32[128]{0:T(128)}, u32[]{:S(2)}) copy-start(f32[128]{0:T(128)} %param.17) | copy-start | bytes 1540
  154.5 4.8 %copy-start.4 = (bf16[7,128,128]{1,2,0:T(8,128)(2,1)S(1)}, bf16[7,128,128]{1,2,0:T(8,128)(2,1)}, u32[]{:S(2)}) copy-start(bf16[7,128,128]{1,2,0:T(8,128)(2,1)} %copy.37) | copy-start | bytes 688132
  156.5 1.9 copy-start.1
  199.5 10.8 %copy-start.2 = (bf16[24,8,8,8,128]{4,3,2,1,0:T(8,128)(2,1)S(1)}, bf16[24,8,8,8,128]{4,3,2,1,0:T(8,128)(2,1)}, u32[]{:S(2)}) copy-start(bf16[24,8,8,8,128]{4,3,2,1,0:T(8,128)(2,1)} %copy-done.1) | copy-start | bytes 9437188
  213.0 24.3 %collective-permute-start.7 = (bf16[24,8,8,128]{3,2,1,0:T(8,128)(2,1)}, bf16[24,8,8,128]{3,2,1,0:T(8,128)(2,1)}, u32[]{:S(2)}, u32[]{:S(2)}) collective-permute-start(bf16[24,8,8,128]{3,2,1,0:T(8,128)(2,1)} %get-tuple-element.37), channel_id=1, source_target_pairs={{0,1},{1,2},{2,3},{3,4},{4,5},{5,6},{6,7},{7,8},{8,9},{9,10},{10,1... | collective-permute-start | bytes 1179656 | tf_op jit(solution)/shard_map/ppermute | solution.py:12
  217.1 24.8 %collective-permute-start.6 = (bf16[24,8,8,128]{3,2,1,0:T(8,128)(2,1)}, bf16[24,8,8,128]{3,2,1,0:T(8,128)(2,1)}, u32[]{:S(2)}, u32[]{:S(2)}) collective-permute-start(bf16[24,8,8,128]{3,2,1,0:T(8,128)(2,1)} %get-tuple-element.38), channel_id=1, source_target_pairs={{1,0},{2,1},{3,2},{4,3},{5,4},{6,5},{7,6},{8,7},{9,8},{10,9},{11,1... | collective-permute-start | bytes 1179656 | tf_op jit(solution)/shard_map/ppermute | solution.py:12
  218.4 28.2 %collective-permute-start.5 = (bf16[24,8,8,128]{3,2,1,0:T(8,128)(2,1)}, bf16[24,8,8,128]{3,2,1,0:T(8,128)(2,1)}, u32[]{:S(2)}, u32[]{:S(2)}) collective-permute-start(bf16[24,8,8,128]{3,2,1,0:T(8,128)(2,1)} %get-tuple-element.39), channel_id=1, source_target_pairs={{0,16},{16,32},{32,48},{48,64},{64,80},{80,96},{96,112},{1,17},{17... | collective-permute-start | bytes 1179656 | tf_op jit(solution)/shard_map/ppermute | solution.py:12
  222.9 35.2 %collective-permute-start.4 = (bf16[24,8,8,128]{3,2,1,0:T(8,128)(2,1)S(1)}, bf16[24,8,8,128]{3,2,1,0:T(8,128)(2,1)}, u32[]{:S(2)}, u32[]{:S(2)}) collective-permute-start(bf16[24,8,8,128]{3,2,1,0:T(8,128)(2,1)S(1)} %get-tuple-element.40), channel_id=1, source_target_pairs={{16,0},{32,16},{48,32},{64,48},{80,64},{96,80},{112,96},{17,1},{33... | collective-permute-start | bytes 1179656 | tf_op jit(solution)/shard_map/ppermute | solution.py:12
  291.0 7.2 %copy-start.5 = (bf16[2,2,2,128,128]{4,3,2,1,0:T(8,128)(2,1)S(1)}, bf16[2,2,2,128,128]{4,3,2,1,0:T(8,128)(2,1)}, u32[]{:S(2)}) copy-start(bf16[2,2,2,128,128]{4,3,2,1,0:T(8,128)(2,1)} %param.19) | copy-start | bytes 786436
  291.0 69.0 %all-to-all-start.1 = ((bf16[16,2,512,128]{3,2,1,0:T(8,128)(2,1)}), bf16[16,2,512,128]{3,2,1,0:T(8,128)(2,1)}, u32[]{:S(2)}, u32[]{:S(2)}) async-start(bf16[16,2,512,128]{3,2,1,0:T(8,128)(2,1)} %broadcast_select_fusion), calls=%async_computation.1 | async-start | bytes 8388608 | tf_op jit(solution)/shard_map/all_to_all | solution.py:139
where the time goes:
time: 456 us; the launch traced here: 449 us
  local copies, waits for them, and re-layouts  198 us (43%)
  other arithmetic  79.2 us (17%)
  matrix products  71.1 us (16%)
  waiting for transfers between devices  60.1 us (13%)
  starting transfers between devices  40.3 us (9%)
    all_to_all x1, waiting for transfers between devices, per_device(): lax.all_to_all(payload, 'gy', split_axis=0, concat_axis=0, tiled=True)  60.1 us
    reshape x1, local copies, waits for them, and re-layouts, subdivide(): product.reshape(count_blocks, 2, half, 2, half, 2, half, 2, 2, 2, channels)  40.5 us
    dot_general x2, matrix products, taps(): jnp.dot(active.reshape(-1, channels), stacked, preferred_element_type=jnp...  36.9 us
    slice x3, local copies, waits for them, and re-layouts, taps(): inner = lax.slice_in_dim(part, 0, edge - 1, axis=axis)  32.7 us
    slice x3, local copies, waits for them, and re-layouts, taps(): inner = lax.slice_in_dim(part, 1, edge, axis=axis)  32.7 us
    transpose x1, local copies, waits for them, and re-layouts, subdivide(): product = product.transpose(0, 1, 3, 5, 2, 7, 4, 8, 6, 9, 10)  29 us
    gather x12, local copies, waits for them, and re-layouts, choose(): jnp.take(candidates, jnp.clip(offset, 0, candidates.shape[0] - 1), axis=0)  27.9 us
    ppermute x8, starting transfers between devices, shifted_2(): return lax.ppermute(block, axis, route)  24 us
  transfers between devices with their start and end apart: 10, of which 1 were waited for; matrix products, arithmetic and copies ran while one was open for 55% of the time, Pallas kernels for 0%

commit v1 on v0

v1 whole, which is shorter than its diff:
```python
import jax
import jax.numpy as jnp
from jax import lax
from jax.experimental import pallas as pl
from jax.experimental.pallas import tpu as pltpu
from jax.sharding import PartitionSpec as P

MESH = pl.DeviceIdType.MESH
BF = jnp.bfloat16
F32 = jnp.float32
S = 24
C = 128
CELLS = 512
LAYER = 64
GROUPS = 4
GS = S // GROUPS
CHUNKS = 4
CR = CELLS // CHUNKS
LIMIT = 60 * 2**20


def dot(a, b):
    return jnp.dot(a, b, preferred_element_type=F32)


def silu_norm(m, half_gain):
    scale = lax.rsqrt(jnp.mean(m * m, axis=-1, keepdims=True) + 1e-6)
    h = m * scale * half_gain
    return (h + h * jnp.tanh(h)).astype(BF)


def branch_kernel(
    lat, g1, k1, g2, k2, owner, slot, dest, out,
    first, second, yl1, yh1, yl2, yh2,
    ra0, ra1, ra2, ra3, rb0, rb1, rb2, rb3,
    mixed, weights, send_sem, recv_sem,
):
    gx = lax.axis_index("gx")
    gy = lax.axis_index("gy")
    n_gx = lax.axis_size("gx")
    n_gy = lax.axis_size("gy")
    me = gx * n_gy + gy
    west = (lax.rem(gx + n_gx - 1, n_gx), gy)
    east = (lax.rem(gx + 1, n_gx), gy)
    south = (gx, lax.rem(gy + n_gy - 1, n_gy))
    north = (gx, lax.rem(gy + 1, n_gy))
    targets = (west, east, south, north)

    barrier = pltpu.get_barrier_semaphore()
    for t in targets:
        pl.semaphore_signal(barrier, inc=1, device_id=t, device_id_type=MESH)

    zero = jnp.zeros((LAYER, C), BF)
    for buf in (yl1, yh1, yl2, yh2, ra0, ra1, ra2, ra3, rb0, rb1, rb2, rb3):
        buf[S] = zero
    for buf in (first, second):
        for q in range(8):
            buf[S, q * LAYER : (q + 1) * LAYER] = zero

    recv = ((ra0, ra1, ra2, ra3), (rb0, rb1, rb2, rb3))
    acts = (first, second)
    y_lo = (yl1, yl2)
    y_hi = (yh1, yh2)
    gains = (g1, g2)
    taps = (k1, k2)

    def copies(n, g):
        blocks = pl.ds(g * GS, GS)
        src = (
            acts[n].at[blocks, pl.ds(0, LAYER)],
            acts[n].at[blocks, pl.ds(CELLS - LAYER, LAYER)],
            y_lo[n].at[blocks],
            y_hi[n].at[blocks],
        )
        return [
            pltpu.make_async_remote_copy(
                src_ref=src[i],
                dst_ref=recv[n][i].at[blocks],
                send_sem=send_sem.at[n, i, g],
                recv_sem=recv_sem.at[n, i, g],
                device_id=targets[i],
                device_id_type=MESH,
            )
            for i in range(4)
        ]

    def emit(n, b, q, m):
        act = silu_norm(m, gains[n][...] * 0.5)
        acts[n][b, q * 128 : (q + 1) * 128] = act
        return act

    def emit_y(n, b, q, m, half_gain):
        h0 = silu_norm_f32(m, half_gain)
        acts[n][b, q * 128 : (q + 1) * 128] = h0.astype(BF)
        y_lo[n][b, q * 16 : (q + 1) * 16] = jnp.concatenate([h0[0:8], h0[64:72]], 0).astype(BF)
        y_hi[n][b, q * 16 : (q + 1) * 16] = jnp.concatenate([h0[56:64], h0[120:128]], 0).astype(BF)

    def silu_norm_f32(m, half_gain):
        scale = lax.rsqrt(jnp.mean(m * m, axis=-1, keepdims=True) + 1e-6)
        h = m * scale * half_gain
        return h + h * jnp.tanh(h)

    def local_slot(b, f):
        s = slot[b, f]
        return jnp.where((s >= 0) & (owner[b, f] == me), s, S)

    def remote_slot(b, f):
        s = slot[b, f]
        return jnp.where((s >= 0) & (owner[b, f] != me), s, S)

    half_1 = g1[...] * 0.5

    def norm_group(g, carry):
        def one(b, carry):
            for q in range(4):
                emit_y(0, b, q, lat[b, q * 128 : (q + 1) * 128].astype(F32), half_1)
            return carry

        lax.fori_loop(g * GS, (g + 1) * GS, one, 0)
        for c in copies(0, g):
            c.start()
        return carry

    pl.semaphore_wait(barrier, 4)
    lax.fori_loop(0, GROUPS, norm_group, 0)

    for n in range(2):
        k = taps[n]
        z = jnp.zeros((C, C), BF)
        tiles = (
            ((k[0], k[3]), (k[1], z)),
            ((z, k[4]), (k[2], z)),
            ((k[5], z), (z, k[6])),
            ((k[1], z), (z, k[2])),
            ((k[3], z), (z, k[4])),
        )
        for w in range(5):
            for r in range(2):
                for c in range(2):
                    weights[n, w, r * C : (r + 1) * C, c * C : (c + 1) * C] = tiles[w][r][c]

    row = lax.broadcasted_iota(jnp.int32, (128, C), 0) % 8
    low = jnp.where(row == 0, 1.0, 0.0).astype(BF)
    not_low = jnp.where(row == 0, 0.0, 1.0).astype(BF)
    high = jnp.where(row == 7, 1.0, 0.0).astype(BF)
    not_high = jnp.where(row == 7, 0.0, 1.0).astype(BF)

    def inner(n, b):
        v = acts[n]
        up = local_slot(b, 4)
        down = local_slot(b, 5)
        zero8 = jnp.zeros((8, C), F32)
        for q in range(4):
            lo, hi = q * 128, (q + 1) * 128
            here = v[b, lo:hi]
            after = v[b, lo + 64 : hi + 64] if q < 3 else jnp.concatenate([v[b, lo + 64 : hi], zero], 0)
            before = v[b, lo - 64 : hi - 64] if q > 0 else jnp.concatenate([zero, v[b, lo : hi - 64]], 0)
            a = dot(jnp.concatenate([here, after], 1), weights[n, 0])
            p = dot(jnp.concatenate([here, before], 1), weights[n, 1])
            z_up = here * not_low + v[up, lo:hi] * low
            z_down = here * not_high + v[down, lo:hi] * high
            z = dot(jnp.concatenate([z_up, z_down], 1), weights[n, 2])
            total = a[:, :C] + p[:, :C]
            total += pltpu.roll(z[:, :C].reshape(16, 8, C), 7, 1).reshape(128, C)
            total += pltpu.roll(z[:, C:].reshape(16, 8, C), 1, 1).reshape(128, C)
            yp, ym = a[:, C:], p[:, C:]
            total += jnp.concatenate([yp[8:64], zero8, yp[72:128], zero8], 0)
            total += jnp.concatenate([zero8, ym[0:56], zero8, ym[64:120]], 0)
            mixed[b, lo:hi] = total

    def faces(n, b):
        v, r = acts[n], recv[n]
        x_pair = jnp.concatenate(
            [
                v[local_slot(b, 0), 0:LAYER] + r[0][remote_slot(b, 0)],
                v[local_slot(b, 1), CELLS - LAYER : CELLS] + r[1][remote_slot(b, 1)],
            ],
            1,
        )
        y_pair = jnp.concatenate(
            [
                y_lo[n][local_slot(b, 2)] + r[2][remote_slot(b, 2)],
                y_hi[n][local_slot(b, 3)] + r[3][remote_slot(b, 3)],
            ],
            1,
        )
        return dot(x_pair, weights[n, 3]), dot(y_pair, weights[n, 4])

    def whole(b, q, fx, fy):
        m = mixed[b, q * 128 : (q + 1) * 128]
        lo, hi = fy[q * 16 : (q + 1) * 16, C:], fy[q * 16 : (q + 1) * 16, :C]
        m0, m1 = m[0:64], m[64:128]
        if q == 0:
            m0 = m0 + fx[:, C:]
        if q == 3:
            m1 = m1 + fx[:, :C]
        return jnp.concatenate(
            [
                m0[0:8] + lo[0:8], m0[8:56], m0[56:64] + hi[0:8],
                m1[0:8] + lo[8:16], m1[8:56], m1[56:64] + hi[8:16],
            ],
            0,
        )

    def run_inner(n):
        def one(b, carry):
            inner(n, b)
            return carry

        lax.fori_loop(0, S, one, 0)

    def wait_faces(n):
        def one(g, carry):
            for c in copies(n, g):
                c.wait_recv()
            return carry

        lax.fori_loop(0, GROUPS, one, 0)

    run_inner(0)
    wait_faces(0)

    half_2 = g2[...] * 0.5

    def second_group(g, carry):
        def one(b, carry):
            fx, fy = faces(0, b)
            for q in range(4):
                emit_y(1, b, q, whole(b, q, fx, fy), half_2)
            return carry

        lax.fori_loop(g * GS, (g + 1) * GS, one, 0)
        for c in copies(1, g):
            c.start()
        return carry

    lax.fori_loop(0, GROUPS, second_group, 0)
    run_inner(1)
    wait_faces(1)

    base = dest[0, 0]

    def hidden_one(p, carry):
        y = gy + p // 6
        b = ((y - base) & 3) + 4 * (p % 6)
        fx, fy = faces(1, b)
        for q in range(4):
            rows = slice(q * 128, (q + 1) * 128)
            out[p, rows] = (lat[b, rows].astype(F32) + whole(b, q, fx, fy)).astype(BF)
        return carry

    lax.fori_loop(0, S, hidden_one, 0)

    def finish(g, carry):
        for n in range(2):
            for c in copies(n, g):
                c.wait_send()
        return carry

    lax.fori_loop(0, GROUPS, finish, 0)


def branch(lat, g1, k1, g2, k2, owner, slot, dest):
    vm = pl.BlockSpec(memory_space=pltpu.VMEM)
    sm = pl.BlockSpec(memory_space=pltpu.SMEM)
    layer = pltpu.VMEM((S + 1, LAYER, C), BF)
    return pl.pallas_call(
        branch_kernel,
        out_shape=jax.ShapeDtypeStruct((S, CELLS, C), BF),
        in_specs=[vm, vm, vm, vm, vm, sm, sm, sm],
        out_specs=vm,
        scratch_shapes=[
            pltpu.VMEM((S + 1, CELLS, C), BF),
            pltpu.VMEM((S + 1, CELLS, C), BF),
            *([layer] * 12),
            pltpu.VMEM((S, CELLS, C), F32),
            pltpu.VMEM((2, 5, 2 * C, 2 * C), BF),
            pltpu.SemaphoreType.DMA((2, 4, GROUPS)),
            pltpu.SemaphoreType.DMA((2, 4, GROUPS)),
        ],
        compiler_params=pltpu.CompilerParams(
            collective_id=0, has_side_effects=True, vmem_limit_bytes=LIMIT
        ),
        cost_estimate=pl.CostEstimate(flops=7 * 10**9, bytes_accessed=8 * 10**6, transcendentals=6 * 10**6),
        name="branch",
    )(lat, g1, k1, g2, k2, owner, slot, dest)


def spread_kernel(hid, table, out, index, *scratch):
    came = scratch[:CHUNKS]
    ready = scratch[CHUNKS : 2 * CHUNKS]
    ys, yr, zs, zr, own = scratch[2 * CHUNKS :]
    gx = lax.axis_index("gx")
    gy = lax.axis_index("gy")
    z, y = gy // 4, gy % 4

    def along_y(d):
        return (gx, z * 4 + lax.rem(y + d, 4))

    def along_z(d):
        return (gx, lax.rem(z + d, 4) * 4 + y)

    barrier = pltpu.get_barrier_semaphore()
    for d in range(1, 4):
        pl.semaphore_signal(barrier, inc=1, device_id=along_y(d), device_id_type=MESH)
        pl.semaphore_signal(barrier, inc=1, device_id=along_z(d), device_id_type=MESH)
    pl.semaphore_wait(barrier, 6)

    def y_copy(c, d):
        rows = pl.ds(c * CR, CR)
        return pltpu.make_async_remote_copy(
            src_ref=hid.at[pl.ds(6 * d, 6), rows],
            dst_ref=came[c].at[pl.ds(6 * d, 6)],
            send_sem=ys.at[c, d],
            recv_sem=yr.at[c, d],
            device_id=along_y(d),
            device_id_type=MESH,
        )

    def z_copy(c, d):
        return pltpu.make_async_remote_copy(
            src_ref=ready[c].at[pl.ds(6 * d, 6)],
            dst_ref=out.at[pl.ds(6 * d, 6), pl.ds(c * CR, CR)],
            send_sem=zs.at[c, d],
            recv_sem=zr.at[c, d],
            device_id=along_z(d),
            device_id_type=MESH,
        )

    def own_copy(c):
        return pltpu.make_async_copy(
            ready[c].at[pl.ds(0, 6)], out.at[pl.ds(0, 6), pl.ds(c * CR, CR)], own.at[c]
        )

    for c in range(CHUNKS):
        for d in range(1, 4):
            y_copy(c, d).start()

    def count(g):
        def one(s, n):
            return n + jnp.where(table[g, s] >= 0, 1, 0)

        return lax.fori_loop(0, S, one, 0)

    def of_class(g):
        n = count(g)
        return (n - ((y - table[g, 0]) & 3) + 3) // 4, n

    here = 4 * z
    ends = []
    total = 0
    for k in range(4):
        m, _ = of_class(here + k)
        total = total + m
        ends.append(total)
    starts = [0] + ends[:3]
    z_first = 0
    for k in reversed(range(4)):
        first_slot = (y - table[here + k, 0]) & 3
        d = table[here + k, 0] + first_slot
        z_k = (d // 4) & 3
        z_first = jnp.where(ends[k] - starts[k] > 0, z_k, z_first)

    def pick(p):
        q = ((z + p // 6 - z_first) & 3) + 4 * (p % 6)
        q = jnp.minimum(q, jnp.maximum(total - 1, 0))
        k = jnp.where(q >= ends[0], 1, 0) + jnp.where(q >= ends[1], 1, 0) + jnp.where(q >= ends[2], 1, 0)
        begin = jnp.where(k == 0, starts[0], jnp.where(k == 1, starts[1], jnp.where(k == 2, starts[2], starts[3])))
        return ((y - k) & 3) * 6 + jnp.minimum(q - begin, 5)

    arriving = []
    for k in range(4):
        n_all = 0
        base = 0
        for g in reversed(range(4)):
            n = count(4 * k + g)
            n_all = n_all + n
            base = jnp.where(n > 0, table[4 * k + g, 0], base)
        arriving.append((n_all - ((gy - base) & 15) + 15) // 16)

    def index_one(t, carry):
        at, begin = S, 0
        for k in range(4):
            inside = (t >= begin) & (t < begin + arriving[k])
            at = jnp.where(inside, ((z - k) & 3) * 6 + t - begin, at)
            begin = begin + arriving[k]
        index[t] = at
        return carry

    lax.fori_loop(0, S, index_one, 0)

    for c in range(CHUNKS):
        came[c][0:6] = hid[0:6, c * CR : (c + 1) * CR]
        for d in range(1, 4):
            y_copy(c, d).wait_recv()

        def gather(p, carry):
            ready[c][p] = came[c][pick(p)]
            return carry

        lax.fori_loop(0, S, gather, 0)
        for d in range(1, 4):
            z_copy(c, d).start()
        own_copy(c).start()
    for c in range(CHUNKS):
        own_copy(c).wait()
        for d in range(1, 4):
            y_copy(c, d).wait_send()
            z_copy(c, d).wait_send()
            z_copy(c, d).wait_recv()


def spread(hid, table):
    part = pltpu.VMEM((S, CR, C), BF)
    return pl.pallas_call(
        spread_kernel,
        out_shape=(
            jax.ShapeDtypeStruct((S, CELLS, C), BF),
            jax.ShapeDtypeStruct((S,), jnp.int32),
        ),
        in_specs=[pl.BlockSpec(memory_space=pltpu.VMEM), pl.BlockSpec(memory_space=pltpu.SMEM)],
        out_specs=(pl.BlockSpec(memory_space=pl.ANY), pl.BlockSpec(memory_space=pltpu.SMEM)),
        scratch_shapes=[
            *([part] * (2 * CHUNKS)),
            *([pltpu.SemaphoreType.DMA((CHUNKS, 4))] * 4),
            pltpu.SemaphoreType.DMA((CHUNKS,)),
        ],
        compiler_params=pltpu.CompilerParams(
            collective_id=1, has_side_effects=True, vmem_limit_bytes=LIMIT
        ),
        name="spread",
    )(hid, table)


def raise_kernel(index, moved, up, out, wide, weights):
    t = pl.program_id(0)

    @pl.when(t == 0)
    def _():
        for o1 in range(2):
            for o2 in range(2):
                for o3 in range(2):
                    weights[o1, o3 * C : (o3 + 1) * C, o2 * C : (o2 + 1) * C] = up[o1, o2, o3]

    at = index[t]
    keep = jnp.where(at < S, 1.0, 0.0)
    parity = lax.broadcasted_iota(jnp.int32, (128, C), 0) % 2
    even = jnp.where(parity == 0, keep, 0.0).astype(BF)
    odd = jnp.where(parity == 1, keep, 0.0).astype(BF)
    for i in range(8):
        v = moved[0, i * 64 : (i + 1) * 64].astype(F32)
        wide[i, pl.ds(0, 64, stride=2)] = v
        wide[i, pl.ds(1, 64, stride=2)] = v
        twice = wide[i].astype(BF)
        lhs = jnp.concatenate([twice * even, twice * odd], 1)
        for o1 in range(2):
            r = dot(lhs, weights[o1])
            r0 = r[:, :C].reshape(2, 4, 2, 8, C)
            r1 = r[:, C:].reshape(2, 4, 2, 8, C)
            both = jnp.concatenate([r0, r1], 3).astype(BF)
            a, u = i // 4, 2 * (i % 4) + o1
            for b in range(2):
                for m in range(2):
                    out[4 * a + 2 * b + m, u * 64 : (u + 1) * 64] = both[b, :, m].reshape(64, C)


def raise_(index, moved, up):
    def block_of(t, index):
        return (jnp.minimum(index[t], S - 1), 0, 0)

    return pl.pallas_call(
        raise_kernel,
        out_shape=jax.ShapeDtypeStruct((8 * S, CELLS, C), BF),
        grid_spec=pltpu.PrefetchScalarGridSpec(
            num_scalar_prefetch=1,
            grid=(S,),
            in_specs=[
                pl.BlockSpec((1, CELLS, C), block_of),
                pl.BlockSpec((2, 2, 2, C, C), lambda t, index: (0, 0, 0, 0, 0)),
            ],
            out_specs=pl.BlockSpec((8, CELLS, C), lambda t, index: (t, 0, 0)),
            scratch_shapes=[pltpu.VMEM((8, 128, C), F32), pltpu.VMEM((2, 2 * C, 2 * C), BF)],
        ),
        compiler_params=pltpu.CompilerParams(
            dimension_semantics=("arbitrary",), vmem_limit_bytes=LIMIT
        ),
        name="raise",
    )(index, moved, up)


def per_device(
    latents, gain_first, conv_first, gain_second, conv_second, upward,
    neighbour_owner, neighbour_slot, destination_device, destination_slot,
):
    lat = latents.reshape(S, CELLS, C)
    dest = destination_device.reshape(1, S)
    table = lax.all_gather(destination_device.reshape(S), "gy")
    packed = branch(
        lat, gain_first.reshape(1, C), conv_first, gain_second.reshape(1, C), conv_second,
        neighbour_owner.reshape(S, 6), neighbour_slot.reshape(S, 6), dest,
    )
    arrived, index = spread(packed, table)
    children = raise_(index, arrived, upward)
    return children.reshape(1, 1, 8 * S, CELLS, C)


def solution(mesh):
    placed = (
        P("gx", "gy", None, None, None),
        P(), P(), P(), P(), P(),
        P("gx", "gy", None, None),
        P("gx", "gy", None, None),
        P("gx", "gy", None),
        P("gx", "gy", None),
    )
    return jax.shard_map(
        per_device,
        mesh=mesh,
        in_specs=placed,
        out_specs=P("gx", "gy", None, None, None),
        check_vma=False,
    )
```

time: 456 us -> 143 us (0.31); the launches traced: 449 us -> 141 us
  local copies, waits for them, and re-layouts: 198 us -> 2.72 us
  Pallas kernels: 0 us -> 118 us
  other arithmetic: 79.2 us -> 0 us
  matrix products: 71.1 us -> 0 us
  waiting for transfers between devices: 60.1 us -> 0 us
  starting transfers between devices: 40.3 us -> 0 us
  blocking collectives: 0 us -> 20.1 us
    pallas_call x0 -> x3, Pallas kernels: none -> 118 us  [the longest x1 52.6 us: spread(): pl.pallas_call(spread_kernel, out_shape=(jax.ShapeDtypeStruct((S, CELLS,...]
    slice x8 -> x0, local copies, waits for them, and re-layouts: 73.7 us -> none  [the longest x3 32.7 us: taps(): inner = lax.slice_in_dim(part, 0, edge - 1, axis=axis)]
    dot_general x15 -> x0, matrix products: 71.1 us -> none  [the longest x2 36.9 us: taps(): jnp.dot(active.reshape(-1, channels), stacked, preferred_element_type=jnp...]
    all_to_all x2 -> x0, waiting for transfers between devices: 60.1 us -> none  [the longest x1 60.1 us: per_device(): lax.all_to_all(payload, 'gy', split_axis=0, concat_axis=0, tiled=True)]
    reshape x2 -> x0, local copies, waits for them, and re-layouts: 40.6 us -> none  [the longest x1 40.5 us: subdivide(): product.reshape(count_blocks, 2, half, 2, half, 2, half, 2, 2, 2, channels)]
    gather x14 -> x0, local copies, waits for them, and re-layouts: 37.9 us -> none  [the longest x12 27.9 us: choose(): jnp.take(candidates, jnp.clip(offset, 0, candidates.shape[0] - 1), axis=0)]
    transpose x1 -> x0, local copies, waits for them, and re-layouts: 29 us -> none  [subdivide(): product = product.transpose(0, 1, 3, 5, 2, 7, 4, 8, 6, 9, 10)]
    ppermute x8 -> x0, starting transfers between devices: 24 us -> none  [shifted_2(): return lax.ppermute(block, axis, route)]
  transfers between devices with their start and end apart: 10 -> 0, of which waited for: 1 -> 0; matrix products, arithmetic and copies ran while one was open for 55% -> 0% of each run, Pallas kernels for 0% -> 0%
where the time goes in v1:
time: 143 us; the launch traced here: 141 us
  Pallas kernels  118 us (83%)
  blocking collectives  20.1 us (14%)
  local copies, waits for them, and re-layouts  2.72 us (2%)
    pallas_call x1, Pallas kernels, spread(): pl.pallas_call(spread_kernel, out_shape=(jax.ShapeDtypeStruct((S, CELLS,...  52.6 us
    pallas_call x1, Pallas kernels, branch(): pl.pallas_call(branch_kernel, out_shape=jax.ShapeDtypeStruct((S, CELLS, C...  44.5 us
    pallas_call x1, Pallas kernels, raise_(): pl.pallas_call(raise_kernel, out_shape=jax.ShapeDtypeStruct((8 * S, CELLS...  21.1 us
    all_gather x1, blocking collectives, per_device(): table = lax.all_gather(destination_device.reshape(S), 'gy')  20.1 us

profile of v1, /device:TPU:1, one launch (start us, length us, event | category | flops | bytes accessed | tf_op | source)
XLA Modules:
  0.0 141.1 jit_solution(985244428282819726)
XLA Ops:
  0.0 20.1 %all-gather = s32[16,1,24]{2,1,0:T(1,128)} all-gather(s32[1,1,24]{2,1,0:T(1,128)} %param.18), channel_id=2, replica_groups=mesh['gx'=8,'gy'=16] {'gy'}, dimensions={0}, use_global_device_ids=true | all-gather | bytes 1632 | tf_op jit(solution)/shard_map/all_gather | solution.py:497
  20.1 1.4 copy.13
  21.5 1.4 copy.14
  22.9 44.5 %branch.1.hid = bf16[24,512,128]{2,1,0:T(8,128)(2,1)} custom-call(bf16[24,512,128]{2,1,0:T(8,128)(2,1)} %bitcast.12, f32[1,128]{1,0:T(1,128)} %bitcast.13, bf16[7,128,128]{2,1,0:T(8,128)(2,1)} %k1.1, f32[1,128]{1,0:T(1,128)} %bitcast.14, bf16[7,128,128]{2,1,0:T(8,128)(2,1)} %k2.1, s32[24,6]{1,0:T(8,128)} %bitcast.9, s32[24,6]{1,0:T(8,128)} %bitcast.10, ...), custom_call_target="tpu_custom_call" | custom-call | flops 7000000000 | bytes 8000000 | tf_op jit(solution)/shard_map/branch/pallas_call | solution.py:267
  67.4 52.6 %spread.1 = (bf16[24,512,128]{2,1,0:T(8,128)(2,1)}, s32[24]{0:T(128)}) custom-call(bf16[24,512,128]{2,1,0:T(8,128)(2,1)} %branch.1.hid, s32[16,24]{1,0:T(8,128)} %bitcast.8), custom_call_target="tpu_custom_call" | custom-call | tf_op jit(solution)/shard_map/spread/pallas_call | solution.py:415
  120.0 21.1 %raise.1 = bf16[192,512,128]{2,1,0:T(8,128)(2,1)} custom-call(s32[24]{0:T(128)} %get-tuple-element.7.index, bf16[24,512,128]{2,1,0:T(8,128)(2,1)} %get-tuple-element.8.moved, bf16[2,2,2,128,128]{4,3,2,1,0:T(8,128)(2,1)} %up.1), custom_call_target="tpu_custom_call" | custom-call | tf_op jit(solution)/shard_map/raise/pallas_call | solution.py:471

commit v2 on v1

v2 whole, which is shorter than its diff:
```python
import jax
import jax.numpy as jnp
from jax import lax
from jax.experimental import pallas as pl
from jax.experimental.pallas import tpu as pltpu
from jax.sharding import PartitionSpec as P

MESH = pl.DeviceIdType.MESH
BF = jnp.bfloat16
F32 = jnp.float32
S = 24
C = 128
CELLS = 512
LAYER = 64
GROUPS = 4
GS = S // GROUPS
CHUNKS = 8
CR = CELLS // CHUNKS
LIMIT = 60 * 2**20


def dot(a, b):
    return jnp.dot(a, b, preferred_element_type=F32)


def main_kernel(lat_hbm, g1, k1, g2, k2, owner, slot, dest, out, index, *scratch):
    (
        lat, first, second, yl1, yh1, yl2, yh2,
        ra0, ra1, ra2, ra3, rb0, rb1, rb2, rb3,
        mixed, weights, face_x, face_y, hid, tabs, tab, picks,
        lat_sem, send_sem, recv_sem, tab_send, tab_recv, tab_sem,
        ys, yr, zs, zr, own,
    ) = scratch[: -2 * CHUNKS]
    came = scratch[-2 * CHUNKS : -CHUNKS]
    ready = scratch[-CHUNKS:]
    gx = lax.axis_index("gx")
    gy = lax.axis_index("gy")
    n_gx = lax.axis_size("gx")
    n_gy = lax.axis_size("gy")
    me = gx * n_gy + gy
    z, y = gy // 4, gy % 4
    targets = (
        (lax.rem(gx + n_gx - 1, n_gx), gy),
        (lax.rem(gx + 1, n_gx), gy),
        (gx, lax.rem(gy + n_gy - 1, n_gy)),
        (gx, lax.rem(gy + 1, n_gy)),
    )

    def along_y(d):
        return (gx, z * 4 + lax.rem(y + d, 4))

    def along_z(d):
        return (gx, lax.rem(z + d, 4) * 4 + y)

    barrier = pltpu.get_barrier_semaphore()
    for t in targets:
        pl.semaphore_signal(barrier, inc=1, device_id=t, device_id_type=MESH)
    for d in range(1, 4):
        pl.semaphore_signal(barrier, inc=1, device_id=along_y(d), device_id_type=MESH)
        pl.semaphore_signal(barrier, inc=1, device_id=along_z(d), device_id_type=MESH)

    def fetch(g):
        part = pl.ds(g * GS, GS)
        return pltpu.make_async_copy(lat_hbm.at[part], lat.at[part], lat_sem.at[g])

    for g in range(GROUPS):
        fetch(g).start()

    zero = jnp.zeros((LAYER, C), BF)
    for buf in (yl1, yh1, yl2, yh2, ra0, ra1, ra2, ra3, rb0, rb1, rb2, rb3):
        buf[S] = zero
    for buf in (first, second):
        for q in range(8):
            buf[S, q * LAYER : (q + 1) * LAYER] = zero

    recv = ((ra0, ra1, ra2, ra3), (rb0, rb1, rb2, rb3))
    acts = (first, second)
    y_lo = (yl1, yl2)
    y_hi = (yh1, yh2)
    taps = (k1, k2)

    for n in range(2):
        k = taps[n]
        o = jnp.zeros((C, C), BF)
        tiles = (
            ((k[0], k[3]), (k[1], o)),
            ((o, k[4]), (k[2], o)),
            ((k[5], o), (o, k[6])),
            ((k[1], o), (o, k[2])),
            ((k[3], o), (o, k[4])),
        )
        for w in range(5):
            for r in range(2):
                for c in range(2):
                    weights[n, w, r * C : (r + 1) * C, c * C : (c + 1) * C] = tiles[w][r][c]

    def copies(n, g):
        blocks = pl.ds(g * GS, GS)
        src = (
            acts[n].at[blocks, pl.ds(0, LAYER)],
            acts[n].at[blocks, pl.ds(CELLS - LAYER, LAYER)],
            y_lo[n].at[blocks],
            y_hi[n].at[blocks],
        )
        return [
            pltpu.make_async_remote_copy(
                src_ref=src[i],
                dst_ref=recv[n][i].at[blocks],
                send_sem=send_sem.at[n, i, g],
                recv_sem=recv_sem.at[n, i, g],
                device_id=targets[i],
                device_id_type=MESH,
            )
            for i in range(4)
        ]

    def emit(n, b, q, m, half_gain):
        scale = lax.rsqrt(jnp.mean(m * m, axis=-1, keepdims=True) + 1e-6)
        h = m * scale * half_gain
        act = h + h * jnp.tanh(h)
        acts[n][b, q * 128 : (q + 1) * 128] = act.astype(BF)
        y_lo[n][b, q * 16 : (q + 1) * 16] = jnp.concatenate([act[0:8], act[64:72]], 0).astype(BF)
        y_hi[n][b, q * 16 : (q + 1) * 16] = jnp.concatenate([act[56:64], act[120:128]], 0).astype(BF)

    def local_slot(b, f):
        s = slot[f, 0, b]
        return jnp.where((s >= 0) & (owner[f, 0, b] == me), s, S)

    def remote_slot(b, f):
        s = slot[f, 0, b]
        return jnp.where((s >= 0) & (owner[f, 0, b] != me), s, S)

    def count(s, n):
        return n + jnp.where(dest[0, s] >= 0, 1, 0)

    base = dest[0, 0]
    held = lax.fori_loop(0, S, count, 0)
    lane = lax.broadcasted_iota(jnp.int32, (8, C), 1)
    tabs[0] = jnp.where(lane == 0, held, base)

    def tab_copy(k, d):
        if k == 0:
            src, dst, to = tabs.at[0], tabs.at[d], along_y(d)
        else:
            src, dst, to = tabs.at[pl.ds(0, 4)], tabs.at[pl.ds(4 * d, 4)], along_z(d)
        return pltpu.make_async_remote_copy(
            src_ref=src,
            dst_ref=dst,
            send_sem=tab_send.at[k, d],
            recv_sem=tab_recv.at[k, d],
            device_id=to,
            device_id_type=MESH,
        )

    half_1 = g1[...] * 0.5

    def norm_group(g, carry):
        fetch(g).wait()

        def one(b, carry):
            for q in range(4):
                emit(0, b, q, lat[b, q * 128 : (q + 1) * 128].astype(F32), half_1)
            return carry

        lax.fori_loop(0, GS, lambda t, k: one(g * GS + t, k), 0, unroll=2)
        for c in copies(0, g):
            c.start()
        return carry

    pl.semaphore_wait(barrier, 10)
    for d in range(1, 4):
        tab_copy(0, d).start()
    lax.fori_loop(0, GROUPS, norm_group, 0)
    for d in range(1, 4):
        tab_copy(0, d).wait()
    for d in range(1, 4):
        tab_copy(1, d).start()

    row = lax.broadcasted_iota(jnp.int32, (128, C), 0) % 8
    low = jnp.where(row == 0, 1.0, 0.0).astype(BF)
    not_low = jnp.where(row == 0, 0.0, 1.0).astype(BF)
    high = jnp.where(row == 7, 1.0, 0.0).astype(BF)
    not_high = jnp.where(row == 7, 0.0, 1.0).astype(BF)

    def inner(n, b):
        v = acts[n]
        up = local_slot(b, 4)
        down = local_slot(b, 5)
        zero8 = jnp.zeros((8, C), F32)
        for q in range(4):
            lo, hi = q * 128, (q + 1) * 128
            here = v[b, lo:hi]
            after = v[b, lo + 64 : hi + 64] if q < 3 else jnp.concatenate([v[b, lo + 64 : hi], zero], 0)
            before = v[b, lo - 64 : hi - 64] if q > 0 else jnp.concatenate([zero, v[b, lo : hi - 64]], 0)
            a = dot(jnp.concatenate([here, after], 1), weights[n, 0])
            p = dot(jnp.concatenate([here, before], 1), weights[n, 1])
            z_up = here * not_low + v[up, lo:hi] * low
            z_down = here * not_high + v[down, lo:hi] * high
            w = dot(jnp.concatenate([z_up, z_down], 1), weights[n, 2])
            total = a[:, :C] + p[:, :C]
            total += pltpu.roll(w[:, :C].reshape(16, 8, C), 7, 1).reshape(128, C)
            total += pltpu.roll(w[:, C:].reshape(16, 8, C), 1, 1).reshape(128, C)
            yp, ym = a[:, C:], p[:, C:]
            total += jnp.concatenate([yp[8:64], zero8, yp[72:128], zero8], 0)
            total += jnp.concatenate([zero8, ym[0:56], zero8, ym[64:120]], 0)
            mixed[b, lo:hi] = total

    def faces(n, b):
        v, r = acts[n], recv[n]
        x_pair = jnp.concatenate(
            [
                v[local_slot(b, 0), 0:LAYER] + r[0][remote_slot(b, 0)],
                v[local_slot(b, 1), CELLS - LAYER : CELLS] + r[1][remote_slot(b, 1)],
            ],
            1,
        )
        y_pair = jnp.concatenate(
            [
                y_lo[n][local_slot(b, 2)] + r[2][remote_slot(b, 2)],
                y_hi[n][local_slot(b, 3)] + r[3][remote_slot(b, 3)],
            ],
            1,
        )
        return dot(x_pair, weights[n, 3]), dot(y_pair, weights[n, 4])

    def plane(b, i, fx, fy):
        m = mixed[b, i * 64 : (i + 1) * 64]
        if i == 0:
            m = m + fx[:, C:]
        if i == 7:
            m = m + fx[:, :C]
        return jnp.concatenate([m[0:8] + fy[:, C:], m[8:56], m[56:64] + fy[:, :C]], 0)

    def run_inner(n):
        def one(b, carry):
            inner(n, b)
            return carry

        lax.fori_loop(0, S, one, 0, unroll=2)

    def wait_faces(n):
        def one(g, carry):
            for c in copies(n, g):
                c.wait_recv()
            return carry

        lax.fori_loop(0, GROUPS, one, 0)

    run_inner(0)
    wait_faces(0)

    half_2 = g2[...] * 0.5

    def second_group(g, carry):
        def one(b, carry):
            fx, fy = faces(0, b)
            for q in range(4):
                both = [plane(b, i, fx, fy[8 * i : 8 * i + 8]) for i in (2 * q, 2 * q + 1)]
                emit(1, b, q, jnp.concatenate(both, 0), half_2)
            return carry

        lax.fori_loop(0, GS, lambda t, k: one(g * GS + t, k), 0, unroll=3)
        for c in copies(1, g):
            c.start()
        return carry

    lax.fori_loop(0, GROUPS, second_group, 0)
    run_inner(1)

    def source_of(p):
        return ((y + p // 6 - base) & 3) + 4 * (p % 6)

    wait_faces(1)

    def face_one(p, carry):
        fx, fy = faces(1, source_of(p))
        face_x[p] = fx
        face_y[p] = fy
        return carry

    lax.fori_loop(0, S, face_one, 0, unroll=8)

    def y_copy(c, d):
        return pltpu.make_async_remote_copy(
            src_ref=hid.at[pl.ds(6 * d, 6), pl.ds(c * CR, CR)],
            dst_ref=came[c].at[pl.ds(6 * d, 6)],
            send_sem=ys.at[c, d],
            recv_sem=yr.at[c, d],
            device_id=along_y(d),
            device_id_type=MESH,
        )

    def z_copy(c, d):
        return pltpu.make_async_remote_copy(
            src_ref=ready[c].at[pl.ds(6 * d, 6)],
            dst_ref=out.at[pl.ds(6 * d, 6), pl.ds(c * CR, CR)],
            send_sem=zs.at[c, d],
            recv_sem=zr.at[c, d],
            device_id=along_z(d),
            device_id_type=MESH,
        )

    def own_copy(c):
        return pltpu.make_async_copy(
            ready[c].at[pl.ds(0, 6)], out.at[pl.ds(0, 6), pl.ds(c * CR, CR)], own.at[c]
        )

    planes = CR // 64
    for c in range(CHUNKS):

        def rows_of(p, j):
            i = planes * c + j
            b = source_of(p)
            whole = plane(b, i, face_x[p] if i in (0, 7) else None, face_y[p, 8 * i : 8 * i + 8])
            return (lat[b, i * 64 : (i + 1) * 64].astype(F32) + whole).astype(BF)

        def sent(p, carry):
            for j in range(planes):
                i = planes * c + j
                hid[p, i * 64 : (i + 1) * 64] = rows_of(p, j)
            return carry

        def kept(p, carry):
            for j in range(planes):
                came[c][p, j * 64 : (j + 1) * 64] = rows_of(p, j)
            return carry

        lax.fori_loop(6, S, sent, 0, unroll=6)
        for d in range(1, 4):
            y_copy(c, d).start()
        lax.fori_loop(0, 6, kept, 0, unroll=6)

    for d in range(1, 4):
        tab_copy(1, d).wait()
    tab_local = pltpu.make_async_copy(tabs, tab, tab_sem)
    tab_local.start()
    tab_local.wait()

    def held_by(kz, ky):
        at = ((z - kz) & 3) * 4 + ((y - ky) & 3)
        return tab[at, 0, 0], tab[at, 0, 1]

    ends = []
    total = 0
    z_first = 0
    for k in reversed(range(4)):
        n, b0 = held_by(z, k)
        offset = (y - b0) & 3
        z_first = jnp.where(n > offset, ((b0 + offset) // 4) & 3, z_first)
    for k in range(4):
        n, b0 = held_by(z, k)
        total = total + (n - ((y - b0) & 3) + 3) // 4
        ends.append(total)
    starts = [0] + ends[:3]

    def pick(p):
        q = ((z + p // 6 - z_first) & 3) + 4 * (p % 6)
        q = jnp.minimum(q, jnp.maximum(total - 1, 0))
        k = jnp.where(q >= ends[0], 1, 0) + jnp.where(q >= ends[1], 1, 0) + jnp.where(q >= ends[2], 1, 0)
        begin = jnp.where(k == 0, starts[0], jnp.where(k == 1, starts[1], jnp.where(k == 2, starts[2], starts[3])))
        return ((y - k) & 3) * 6 + jnp.minimum(q - begin, 5)

    arriving = []
    for k in range(4):
        n_all = 0
        b_all = 0
        for j in reversed(range(4)):
            n, b0 = held_by(k, j)
            n_all = n_all + n
            b_all = jnp.where(n > 0, b0, b_all)
        arriving.append((n_all - ((gy - b_all) & 15) + 15) // 16)

    def index_one(t, carry):
        at, begin = S, 0
        for k in range(4):
            inside = (t >= begin) & (t < begin + arriving[k])
            at = jnp.where(inside, ((z - k) & 3) * 6 + t - begin, at)
            begin = begin + arriving[k]
        index[t] = at
        return carry

    lax.fori_loop(0, S, index_one, 0)

    def pick_one(p, carry):
        picks[p] = pick(p)
        return carry

    lax.fori_loop(0, S, pick_one, 0)

    for c in range(CHUNKS):
        for d in range(1, 4):
            y_copy(c, d).wait_recv()

        def gather(p, carry):
            ready[c][p] = came[c][picks[p]]
            return carry

        lax.fori_loop(0, S, gather, 0, unroll=4)
        for d in range(1, 4):
            z_copy(c, d).start()
        own_copy(c).start()

    def finish(g, carry):
        for n in range(2):
            for c in copies(n, g):
                c.wait_send()
        return carry

    lax.fori_loop(0, GROUPS, finish, 0)
    for c in range(CHUNKS):
        own_copy(c).wait()
        for d in range(1, 4):
            y_copy(c, d).wait_send()
            z_copy(c, d).wait_send()
            z_copy(c, d).wait_recv()


def main(lat, g1, k1, g2, k2, owner, slot, dest):
    vm = pl.BlockSpec(memory_space=pltpu.VMEM)
    sm = pl.BlockSpec(memory_space=pltpu.SMEM)
    anywhere = pl.BlockSpec(memory_space=pl.ANY)
    layer = pltpu.VMEM((S + 1, LAYER, C), BF)
    dma = pltpu.SemaphoreType.DMA
    return pl.pallas_call(
        main_kernel,
        out_shape=(
            jax.ShapeDtypeStruct((S, CELLS, C), BF),
            jax.ShapeDtypeStruct((S,), jnp.int32),
        ),
        in_specs=[anywhere, vm, vm, vm, vm, sm, sm, sm],
        out_specs=(anywhere, sm),
        scratch_shapes=[
            pltpu.VMEM((S, CELLS, C), BF),
            pltpu.VMEM((S + 1, CELLS, C), BF),
            pltpu.VMEM((S + 1, CELLS, C), BF),
            *([layer] * 12),
            pltpu.VMEM((S, CELLS, C), F32),
            pltpu.VMEM((2, 5, 2 * C, 2 * C), BF),
            pltpu.VMEM((S, LAYER, 2 * C), F32),
            pltpu.VMEM((S, LAYER, 2 * C), F32),
            pltpu.VMEM((S, CELLS, C), BF),
            pltpu.VMEM((16, 8, C), jnp.int32),
            pltpu.SMEM((16, 8, C), jnp.int32),
            pltpu.SMEM((S,), jnp.int32),
            dma((GROUPS,)),
            dma((2, 4, GROUPS)),
            dma((2, 4, GROUPS)),
            dma((2, 4)),
            dma((2, 4)),
            dma,
            *([dma((CHUNKS, 4))] * 4),
            dma((CHUNKS,)),
            *([pltpu.VMEM((S, CR, C), BF)] * (2 * CHUNKS)),
        ],
        compiler_params=pltpu.CompilerParams(
            collective_id=0, has_side_effects=True, vmem_limit_bytes=LIMIT
        ),
        cost_estimate=pl.CostEstimate(flops=7 * 10**9, bytes_accessed=8 * 10**6, transcendentals=6 * 10**6),
        name="main",
    )(lat, g1, k1, g2, k2, owner, slot, dest)


DEPTH = 4


def raise_kernel(index, moved, up, out, blocks, even, odd, weights, done, in_sem, out_sem):
    def get(t):
        return pltpu.make_async_copy(moved.at[jnp.minimum(index[t], S - 1)], blocks.at[t], in_sem.at[t])

    def put(t):
        return pltpu.make_async_copy(done.at[t % DEPTH], out.at[pl.ds(8 * t, 8)], out_sem.at[t % DEPTH])

    def fetch(t, carry):
        get(t).start()
        return carry

    lax.fori_loop(0, S, fetch, 0)
    for o1 in range(2):
        for o2 in range(2):
            for o3 in range(2):
                weights[o1, o3 * C : (o3 + 1) * C, o2 * C : (o2 + 1) * C] = up[o1, o2, o3]
    even[...] = jnp.zeros_like(even)
    odd[...] = jnp.zeros_like(odd)

    def step(t, carry):
        get(t).wait()

        @pl.when(t >= DEPTH)
        def _():
            put(t - DEPTH).wait()

        keep = index[t] < S
        for i in range(8):
            v = blocks[t, i * 64 : (i + 1) * 64].astype(F32)
            v = jnp.where(keep, v, 0.0)
            even[i, pl.ds(0, 64, stride=2)] = v
            odd[i, pl.ds(1, 64, stride=2)] = v
        for o1 in range(2):
            for h in range(2):
                rows = slice(4 * h, 4 * h + 4)
                lhs = jnp.concatenate(
                    [even[rows].reshape(512, C).astype(BF), odd[rows].reshape(512, C).astype(BF)], 1
                )
                r = dot(lhs, weights[o1])
                for k in range(4):
                    part = r[k * 128 : (k + 1) * 128]
                    r0 = part[:, :C].reshape(2, 4, 2, 8, C)
                    r1 = part[:, C:].reshape(2, 4, 2, 8, C)
                    both = jnp.concatenate([r0, r1], 3).astype(BF)
                    u = 2 * k + o1
                    for b in range(2):
                        for m in range(2):
                            done[t % DEPTH, 4 * h + 2 * b + m, u * 64 : (u + 1) * 64] = both[
                                b, :, m
                            ].reshape(64, C)
        put(t).start()
        return carry

    lax.fori_loop(0, S, step, 0)

    def finish(t, carry):
        put(t).wait()
        return carry

    lax.fori_loop(S - DEPTH, S, finish, 0)


def raise_(index, moved, up):
    return pl.pallas_call(
        raise_kernel,
        out_shape=jax.ShapeDtypeStruct((8 * S, CELLS, C), BF),
        in_specs=[
            pl.BlockSpec(memory_space=pltpu.SMEM),
            pl.BlockSpec(memory_space=pl.ANY),
            pl.BlockSpec(memory_space=pltpu.VMEM),
        ],
        out_specs=pl.BlockSpec(memory_space=pl.ANY),
        scratch_shapes=[
            pltpu.VMEM((S, CELLS, C), BF),
            pltpu.VMEM((8, 128, C), F32),
            pltpu.VMEM((8, 128, C), F32),
            pltpu.VMEM((2, 2 * C, 2 * C), BF),
            pltpu.VMEM((DEPTH, 8, CELLS, C), BF),
            pltpu.SemaphoreType.DMA((S,)),
            pltpu.SemaphoreType.DMA((DEPTH,)),
        ],
        compiler_params=pltpu.CompilerParams(vmem_limit_bytes=LIMIT),
        name="raise",
    )(index, moved, up)


def per_device(
    latents, gain_first, conv_first, gain_second, conv_second, upward,
    neighbour_owner, neighbour_slot, destination_device, destination_slot,
):
    arrived, index = main(
        latents.reshape(S, CELLS, C),
        gain_first.reshape(1, C),
        conv_first,
        gain_second.reshape(1, C),
        conv_second,
        neighbour_owner.reshape(S, 6).T.reshape(6, 1, S),
        neighbour_slot.reshape(S, 6).T.reshape(6, 1, S),
        destination_device.reshape(1, S),
    )
    children = raise_(index, arrived, upward)
    return children.reshape(1, 1, 8 * S, CELLS, C)


def solution(mesh):
    placed = (
        P("gx", "gy", None, None, None),
        P(), P(), P(), P(), P(),
        P("gx", "gy", None, None),
        P("gx", "gy", None, None),
        P("gx", "gy", None),
        P("gx", "gy", None),
    )
    return jax.shard_map(
        per_device,
        mesh=mesh,
        in_specs=placed,
        out_specs=P("gx", "gy", None, None, None),
        check_vma=False,
    )
```

time: 143 us -> 94.3 us (0.66)
  the two profiles are of different devices: /device:TPU:1 before, /device:TPU:2 now
where the time goes in v2:
time: 94.3 us; the launch traced here: 94.1 us
  Pallas kernels  91.6 us (97%)
  local copies, waits for them, and re-layouts  2.54 us (3%)
    pallas_call x1, Pallas kernels, main(): pl.pallas_call(main_kernel, out_shape=(jax.ShapeDtypeStruct((S, CELLS, C)...  77.6 us
    pallas_call x1, Pallas kernels, raise_(): pl.pallas_call(raise_kernel, out_shape=jax.ShapeDtypeStruct((8 * S, CELLS...  13.9 us

profile of v2, /device:TPU:2, one launch (start us, length us, event | category | flops | bytes accessed | tf_op | source)
XLA Modules:
  0.0 94.1 jit_solution(2138935688669200465)
XLA Ops:
  0.0 0.7 copy.15
  0.7 0.6 reshape.31.owner
  1.3 0.7 copy.14
  2.0 0.6 reshape.33.slot
  2.5 77.6 %main.1 = (bf16[24,512,128]{2,1,0:T(8,128)(2,1)}, s32[24]{0:T(128)}) custom-call(bf16[24,512,128]{2,1,0:T(8,128)(2,1)} %bitcast.17, f32[1,128]{1,0:T(1,128)} %bitcast.18, bf16[7,128,128]{2,1,0:T(8,128)(2,1)} %k1.1, f32[1,128]{1,0:T(1,128)} %bitcast.19, bf16[7,128,128]{2,1,0:T(8,128)(2,1)} %k2.1, s32[6,1,24]{2,1,0:T(1,128)} %reshape.31.owner, ...), custom_call_target="tpu_custom_call" | custom-call | flops 7000000000 | bytes 8000000 | tf_op jit(solution)/shard_map/main/pallas_call | solution.py:424
  80.2 13.9 %raise.1 = bf16[192,512,128]{2,1,0:T(8,128)(2,1)} custom-call(s32[24]{0:T(128)} %get-tuple-element.7.index, bf16[24,512,128]{2,1,0:T(8,128)(2,1)} %get-tuple-element.8.moved, bf16[2,2,2,128,128]{4,3,2,1,0:T(8,128)(2,1)} %up.1), custom_call_target="tpu_custom_call" | custom-call | tf_op jit(solution)/shard_map/raise/pallas_call | solution.py:529

commit v3 on v2

--- a/solution.py
+++ b/solution.py
@@ -14,7 +14,7 @@
 LAYER = 64
 GROUPS = 4
 GS = S // GROUPS
-CHUNKS = 8
+CHUNKS = 16
 CR = CELLS // CHUNKS
 LIMIT = 60 * 2**20
 
@@ -23,12 +23,12 @@
     return jnp.dot(a, b, preferred_element_type=F32)
 
 
-def main_kernel(lat_hbm, g1, k1, g2, k2, owner, slot, dest, out, index, *scratch):
+def main_kernel(lat_hbm, g1, k1_hbm, g2, k2_hbm, owner, slot, dest, out, index, *scratch):
     (
-        lat, first, second, yl1, yh1, yl2, yh2,
+        lat, k1, k2, first, second, yl1, yh1, yl2, yh2,
         ra0, ra1, ra2, ra3, rb0, rb1, rb2, rb3,
         mixed, weights, face_x, face_y, hid, tabs, tab, picks,
-        lat_sem, send_sem, recv_sem, tab_send, tab_recv, tab_sem,
+        lat_sem, tap_sem, send_sem, recv_sem, tab_send, tab_recv, tab_sem,
         ys, yr, zs, zr, own,
     ) = scratch[: -2 * CHUNKS]
     came = scratch[-2 * CHUNKS : -CHUNKS]
@@ -65,34 +65,18 @@
 
     for g in range(GROUPS):
         fetch(g).start()
-
-    zero = jnp.zeros((LAYER, C), BF)
-    for buf in (yl1, yh1, yl2, yh2, ra0, ra1, ra2, ra3, rb0, rb1, rb2, rb3):
-        buf[S] = zero
-    for buf in (first, second):
-        for q in range(8):
-            buf[S, q * LAYER : (q + 1) * LAYER] = zero
+    fetch_taps = (
+        pltpu.make_async_copy(k1_hbm, k1, tap_sem.at[0]),
+        pltpu.make_async_copy(k2_hbm, k2, tap_sem.at[1]),
+    )
+    for c in fetch_taps:
+        c.start()
 
     recv = ((ra0, ra1, ra2, ra3), (rb0, rb1, rb2, rb3))
     acts = (first, second)
     y_lo = (yl1, yl2)
     y_hi = (yh1, yh2)
     taps = (k1, k2)
-
-    for n in range(2):
-        k = taps[n]
-        o = jnp.zeros((C, C), BF)
-        tiles = (
-            ((k[0], k[3]), (k[1], o)),
-            ((o, k[4]), (k[2], o)),
-            ((k[5], o), (o, k[6])),
-            ((k[1], o), (o, k[2])),
-            ((k[3], o), (o, k[4])),
-        )
-        for w in range(5):
-            for r in range(2):
-                for c in range(2):
-                    weights[n, w, r * C : (r + 1) * C, c * C : (c + 1) * C] = tiles[w][r][c]
 
     def copies(n, g):
         blocks = pl.ds(g * GS, GS)
@@ -114,13 +98,20 @@
             for i in range(4)
         ]
 
-    def emit(n, b, q, m, half_gain):
+    def strip(ref, b, first_row):
+        return jnp.concatenate([ref[b, 64 * i + first_row : 64 * i + first_row + 16] for i in range(8)], 0)
+
+    def emit(n, b, s, m, half_gain):
         scale = lax.rsqrt(jnp.mean(m * m, axis=-1, keepdims=True) + 1e-6)
         h = m * scale * half_gain
         act = h + h * jnp.tanh(h)
-        acts[n][b, q * 128 : (q + 1) * 128] = act.astype(BF)
-        y_lo[n][b, q * 16 : (q + 1) * 16] = jnp.concatenate([act[0:8], act[64:72]], 0).astype(BF)
-        y_hi[n][b, q * 16 : (q + 1) * 16] = jnp.concatenate([act[56:64], act[120:128]], 0).astype(BF)
+        rounded = act.astype(BF)
+        for i in range(8):
+            acts[n][b, 64 * i + 16 * s : 64 * i + 16 * s + 16] = rounded[16 * i : 16 * i + 16]
+        if s == 0:
+            y_lo[n][b] = jnp.concatenate([act[16 * i : 16 * i + 8] for i in range(8)], 0).astype(BF)
+        if s == 3:
+            y_hi[n][b] = jnp.concatenate([act[16 * i + 8 : 16 * i + 16] for i in range(8)], 0).astype(BF)
 
     def local_slot(b, f):
         s = slot[f, 0, b]
@@ -154,23 +145,54 @@
 
     half_1 = g1[...] * 0.5
 
-    def norm_group(g, carry):
+    def norm_group(g):
         fetch(g).wait()
 
         def one(b, carry):
-            for q in range(4):
-                emit(0, b, q, lat[b, q * 128 : (q + 1) * 128].astype(F32), half_1)
+            for s in range(4):
+                emit(0, b, s, strip(lat, b, 16 * s).astype(F32), half_1)
             return carry
 
         lax.fori_loop(0, GS, lambda t, k: one(g * GS + t, k), 0, unroll=2)
+
+    def norm_and_send(g, carry):
+        norm_group(g)
         for c in copies(0, g):
             c.start()
         return carry
 
+    norm_group(0)
     pl.semaphore_wait(barrier, 10)
+    for c in copies(0, 0):
+        c.start()
     for d in range(1, 4):
         tab_copy(0, d).start()
-    lax.fori_loop(0, GROUPS, norm_group, 0)
+    lax.fori_loop(1, GROUPS, norm_and_send, 0)
+
+    zero = jnp.zeros((LAYER, C), BF)
+    for buf in (yl1, yh1, yl2, yh2, ra0, ra1, ra2, ra3, rb0, rb1, rb2, rb3):
+        buf[S] = zero
+    for buf in (first, second):
+        for q in range(8):
+            buf[S, q * LAYER : (q + 1) * LAYER] = zero
+
+    for c in fetch_taps:
+        c.wait()
+    for n in range(2):
+        k = taps[n]
+        o = jnp.zeros((C, C), BF)
+        tiles = (
+            ((k[0], k[1]), (k[3], o)),
+            ((o, k[2]), (k[4], o)),
+            ((k[5], o), (o, k[6])),
+            ((k[1], o), (o, k[2])),
+            ((k[3], o), (o, k[4])),
+        )
+        for w in range(5):
+            for r in range(2):
+                for c in range(2):
+                    weights[n, w, r * C : (r + 1) * C, c * C : (c + 1) * C] = tiles[w][r][c]
+
     for d in range(1, 4):
         tab_copy(0, d).wait()
     for d in range(1, 4):
@@ -182,81 +204,97 @@
     high = jnp.where(row == 7, 1.0, 0.0).astype(BF)
     not_high = jnp.where(row == 7, 0.0, 1.0).astype(BF)
 
-    def inner(n, b):
+    def inner(n, b, s):
         v = acts[n]
         up = local_slot(b, 4)
         down = local_slot(b, 5)
-        zero8 = jnp.zeros((8, C), F32)
-        for q in range(4):
-            lo, hi = q * 128, (q + 1) * 128
-            here = v[b, lo:hi]
-            after = v[b, lo + 64 : hi + 64] if q < 3 else jnp.concatenate([v[b, lo + 64 : hi], zero], 0)
-            before = v[b, lo - 64 : hi - 64] if q > 0 else jnp.concatenate([zero, v[b, lo : hi - 64]], 0)
-            a = dot(jnp.concatenate([here, after], 1), weights[n, 0])
-            p = dot(jnp.concatenate([here, before], 1), weights[n, 1])
-            z_up = here * not_low + v[up, lo:hi] * low
-            z_down = here * not_high + v[down, lo:hi] * high
-            w = dot(jnp.concatenate([z_up, z_down], 1), weights[n, 2])
-            total = a[:, :C] + p[:, :C]
-            total += pltpu.roll(w[:, :C].reshape(16, 8, C), 7, 1).reshape(128, C)
-            total += pltpu.roll(w[:, C:].reshape(16, 8, C), 1, 1).reshape(128, C)
-            yp, ym = a[:, C:], p[:, C:]
-            total += jnp.concatenate([yp[8:64], zero8, yp[72:128], zero8], 0)
-            total += jnp.concatenate([zero8, ym[0:56], zero8, ym[64:120]], 0)
-            mixed[b, lo:hi] = total
-
-    def faces(n, b):
+        zero8 = jnp.zeros((8, C), BF)
+        zero16 = jnp.zeros((16, C), F32)
+        here = strip(v, b, 16 * s)
+        if s < 3:
+            after = strip(v, b, 16 * s + 8)
+        else:
+            after = jnp.concatenate([x for i in range(8) for x in (v[b, 64 * i + 56 : 64 * i + 64], zero8)], 0)
+        if s > 0:
+            before = strip(v, b, 16 * s - 8)
+        else:
+            before = jnp.concatenate([x for i in range(8) for x in (zero8, v[b, 64 * i : 64 * i + 8])], 0)
+        a = dot(jnp.concatenate([here, after], 1), weights[n, 0])
+        p = dot(jnp.concatenate([here, before], 1), weights[n, 1])
+        z_up = here * not_low + strip(v, up, 16 * s) * low
+        z_down = here * not_high + strip(v, down, 16 * s) * high
+        w = dot(jnp.concatenate([z_up, z_down], 1), weights[n, 2])
+        total = a[:, :C] + p[:, :C]
+        total += pltpu.roll(w[:, :C].reshape(16, 8, C), 7, 1).reshape(128, C)
+        total += pltpu.roll(w[:, C:].reshape(16, 8, C), 1, 1).reshape(128, C)
+        total += jnp.concatenate([a[16:, C:], zero16], 0)
+        total += jnp.concatenate([zero16, p[:112, C:]], 0)
+        mixed[b, 128 * s : 128 * s + 128] = total
+
+    def x_faces(n, b):
         v, r = acts[n], recv[n]
-        x_pair = jnp.concatenate(
+        pair = jnp.concatenate(
             [
                 v[local_slot(b, 0), 0:LAYER] + r[0][remote_slot(b, 0)],
                 v[local_slot(b, 1), CELLS - LAYER : CELLS] + r[1][remote_slot(b, 1)],
             ],
             1,
         )
-        y_pair = jnp.concatenate(
+        return dot(pair, weights[n, 3])
+
+    def y_faces(n, b):
+        r = recv[n]
+        pair = jnp.concatenate(
             [
                 y_lo[n][local_slot(b, 2)] + r[2][remote_slot(b, 2)],
                 y_hi[n][local_slot(b, 3)] + r[3][remote_slot(b, 3)],
             ],
             1,
         )
-        return dot(x_pair, weights[n, 3]), dot(y_pair, weights[n, 4])
-
-    def plane(b, i, fx, fy):
-        m = mixed[b, i * 64 : (i + 1) * 64]
-        if i == 0:
-            m = m + fx[:, C:]
-        if i == 7:
-            m = m + fx[:, :C]
-        return jnp.concatenate([m[0:8] + fy[:, C:], m[8:56], m[56:64] + fy[:, :C]], 0)
-
-    def run_inner(n):
+        return dot(pair, weights[n, 4])
+
+    def whole(b, s, fx, fy):
+        m = mixed[b, 128 * s : 128 * s + 128]
+        pieces = []
+        for i in range(8):
+            even, odd = m[16 * i : 16 * i + 8], m[16 * i + 8 : 16 * i + 16]
+            if i in (0, 7):
+                lanes = slice(C, 2 * C) if i == 0 else slice(0, C)
+                even = even + fx[16 * s : 16 * s + 8, lanes]
+                odd = odd + fx[16 * s + 8 : 16 * s + 16, lanes]
+            if s == 0:
+                even = even + fy[8 * i : 8 * i + 8, C:]
+            if s == 3:
+                odd = odd + fy[8 * i : 8 * i + 8, :C]
+            pieces += [even, odd]
+        return jnp.concatenate(pieces, 0)
+
+    def run_inner(n, strips):
         def one(b, carry):
-            inner(n, b)
+            for s in strips:
+                inner(n, b, s)
             return carry
 
-        lax.fori_loop(0, S, one, 0, unroll=2)
-
-    def wait_faces(n):
+        lax.fori_loop(0, S, one, 0, unroll=12 // len(strips))
+
+    def wait_faces(n, which):
         def one(g, carry):
-            for c in copies(n, g):
+            for c in copies(n, g)[which]:
                 c.wait_recv()
             return carry
 
         lax.fori_loop(0, GROUPS, one, 0)
 
-    run_inner(0)
-    wait_faces(0)
+    run_inner(0, (0, 1, 2, 3))
+    wait_faces(0, slice(0, 4))
 
     half_2 = g2[...] * 0.5
 
     def second_group(g, carry):
         def one(b, carry):
-            fx, fy = faces(0, b)
-            for q in range(4):
-                both = [plane(b, i, fx, fy[8 * i : 8 * i + 8]) for i in (2 * q, 2 * q + 1)]
-                emit(1, b, q, jnp.concatenate(both, 0), half_2)
+            fx, fy = x_faces(0, b), y_faces(0, b)
+            for s in range(4):
+                emit(1, b, s, whole(b, s, fx, fy), half_2)
             return carry
 
         lax.fori_loop(0, GS, lambda t, k: one(g * GS + t, k), 0, unroll=3)
@@ -265,20 +303,17 @@
         return carry
 
     lax.fori_loop(0, GROUPS, second_group, 0)
-    run_inner(1)
 
     def source_of(p):
         return ((y + p // 6 - base) & 3) + 4 * (p % 6)
 
-    wait_faces(1)
-
-    def face_one(p, carry):
-        fx, fy = faces(1, source_of(p))
-        face_x[p] = fx
-        face_y[p] = fy
-        return carry
-
-    lax.fori_loop(0, S, face_one, 0, unroll=8)
+    def x_one(p, carry):
+        face_x[p] = x_faces(1, source_of(p))
+        return carry
+
+    def y_one(p, carry):
+        face_y[p] = y_faces(1, source_of(p))
+        return carry
 
     def y_copy(c, d):
         return pltpu.make_async_remote_copy(
@@ -305,30 +340,35 @@
             ready[c].at[pl.ds(0, 6)], out.at[pl.ds(0, 6), pl.ds(c * CR, CR)], own.at[c]
         )
 
-    planes = CR // 64
-    for c in range(CHUNKS):
-
-        def rows_of(p, j):
-            i = planes * c + j
+    parts = 128 // CR
+
+    def hidden(s):
+        def rows_of(p):
             b = source_of(p)
-            whole = plane(b, i, face_x[p] if i in (0, 7) else None, face_y[p, 8 * i : 8 * i + 8])
-            return (lat[b, i * 64 : (i + 1) * 64].astype(F32) + whole).astype(BF)
+            branch = whole(b, s, face_x[p], face_y[p] if s in (0, 3) else None)
+            return (strip(lat, b, 16 * s).astype(F32) + branch).astype(BF)
 
         def sent(p, carry):
-            for j in range(planes):
-                i = planes * c + j
-                hid[p, i * 64 : (i + 1) * 64] = rows_of(p, j)
+            hid[p, s * 128 : (s + 1) * 128] = rows_of(p)
             return carry
 
         def kept(p, carry):
-            for j in range(planes):
-                came[c][p, j * 64 : (j + 1) * 64] = rows_of(p, j)
+            rows = rows_of(p)
+            for j in range(parts):
+                came[parts * s + j][p] = rows[j * CR : (j + 1) * CR]
             return carry
 
-        lax.fori_loop(6, S, sent, 0, unroll=6)
-        for d in range(1, 4):
-            y_copy(c, d).start()
-        lax.fori_loop(0, 6, kept, 0, unroll=6)
+        lax.fori_loop(6, S, sent, 0, unroll=3)
+        for c in range(parts * s, parts * (s + 1)):
+            for d in range(1, 4):
+                y_copy(c, d).start()
+        lax.fori_loop(0, 6, kept, 0, unroll=3)
+
+    run_inner(1, (1, 2))
+    wait_faces(1, slice(0, 2))
+    lax.fori_loop(0, S, x_one, 0, unroll=8)
+    hidden(1)
+    hidden(2)
 
     for d in range(1, 4):
         tab_copy(1, d).wait()
@@ -387,7 +427,7 @@
 
     lax.fori_loop(0, S, pick_one, 0)
 
-    for c in range(CHUNKS):
+    def relay(c):
         for d in range(1, 4):
             y_copy(c, d).wait_recv()
 
@@ -399,6 +439,19 @@
         for d in range(1, 4):
             z_copy(c, d).start()
         own_copy(c).start()
+
+    order = [parts * s + j for s in (1, 2, 0, 3) for j in range(parts)]
+    run_inner(1, (0, 3))
+    for c in order[:1]:
+        relay(c)
+    wait_faces(1, slice(2, 4))
+    lax.fori_loop(0, S, y_one, 0, unroll=8)
+    hidden(0)
+    for c in order[1:2]:
+        relay(c)
+    hidden(3)
+    for c in order[2:]:
+        relay(c)
 
     def finish(g, carry):
         for n in range(2):
@@ -427,10 +480,12 @@
             jax.ShapeDtypeStruct((S, CELLS, C), BF),
             jax.ShapeDtypeStruct((S,), jnp.int32),
         ),
-        in_specs=[anywhere, vm, vm, vm, vm, sm, sm, sm],
+        in_specs=[anywhere, vm, anywhere, vm, anywhere, sm, sm, sm],
         out_specs=(anywhere, sm),
         scratch_shapes=[
             pltpu.VMEM((S, CELLS, C), BF),
+            pltpu.VMEM((7, C, C), BF),
+            pltpu.VMEM((7, C, C), BF),
             pltpu.VMEM((S + 1, CELLS, C), BF),
             pltpu.VMEM((S + 1, CELLS, C), BF),
             *([layer] * 12),
@@ -443,6 +498,7 @@
             pltpu.SMEM((16, 8, C), jnp.int32),
             pltpu.SMEM((S,), jnp.int32),
             dma((GROUPS,)),
+            dma((2,)),
             dma((2, 4, GROUPS)),
             dma((2, 4, GROUPS)),
             dma((2, 4)),
@@ -491,7 +547,9 @@
 
         keep = index[t] < S
         for i in range(8):
-            v = blocks[t, i * 64 : (i + 1) * 64].astype(F32)
+            v = jnp.concatenate(
+                [blocks[t, 128 * s + 16 * i : 128 * s + 16 * i + 16] for s in range(4)], 0
+            ).astype(F32)
             v = jnp.where(keep, v, 0.0)
             even[i, pl.ds(0, 64, stride=2)] = v
             odd[i, pl.ds(1, 64, stride=2)] = v

time: 94.3 us -> 91.8 us (0.973)
  the two profiles are of different devices: /device:TPU:2 before, /device:TPU:1 now
where the time goes in v3:
time: 91.8 us; the launch traced here: 91.6 us
  Pallas kernels  89.1 us (97%)
  local copies, waits for them, and re-layouts  2.54 us (3%)
    pallas_call x1, Pallas kernels, main(): pl.pallas_call(main_kernel, out_shape=(jax.ShapeDtypeStruct((S, CELLS, C)...  75.2 us
    pallas_call x1, Pallas kernels, raise_(): pl.pallas_call(raise_kernel, out_shape=jax.ShapeDtypeStruct((8 * S, CELLS...  13.8 us

profile of v3, /device:TPU:1, one launch (start us, length us, event | category | flops | bytes accessed | tf_op | source)
XLA Modules:
  0.0 91.6 jit_solution(2681929583250356197)
XLA Ops:
  0.0 0.7 copy.15
  0.7 0.6 reshape.31.owner
  1.3 0.7 copy.14
  2.0 0.6 reshape.33.slot
  2.5 75.2 %main.1 = (bf16[24,512,128]{2,1,0:T(8,128)(2,1)}, s32[24]{0:T(128)}) custom-call(bf16[24,512,128]{2,1,0:T(8,128)(2,1)} %bitcast.17, f32[1,128]{1,0:T(1,128)} %bitcast.18, bf16[7,128,128]{2,1,0:T(8,128)(2,1)} %k1_hbm.1, f32[1,128]{1,0:T(1,128)} %bitcast.19, bf16[7,128,128]{2,1,0:T(8,128)(2,1)} %k2_hbm.1, s32[6,1,24]{2,1,0:T(1,128)} %reshape.31.owner, ...), custom_call_target="tpu_custom_call" | custom-call | flops 7000000000 | bytes 8000000 | tf_op jit(solution)/shard_map/main/pallas_call | solution.py:477
  77.8 13.8 %raise.1 = bf16[192,512,128]{2,1,0:T(8,128)(2,1)} custom-call(s32[24]{0:T(128)} %get-tuple-element.7.index, bf16[24,512,128]{2,1,0:T(8,128)(2,1)} %get-tuple-element.8.moved, bf16[2,2,2,128,128]{4,3,2,1,0:T(8,128)(2,1)} %up.1), custom_call_target="tpu_custom_call" | custom-call | tf_op jit(solution)/shard_map/raise/pallas_call | solution.py:587

commit v4 on v3

--- a/solution.py
+++ b/solution.py
@@ -153,7 +153,7 @@
                 emit(0, b, s, strip(lat, b, 16 * s).astype(F32), half_1)
             return carry
 
-        lax.fori_loop(0, GS, lambda t, k: one(g * GS + t, k), 0, unroll=2)
+        lax.fori_loop(0, GS, lambda t, k: one(g * GS + t, k), 0, unroll=3)
 
     def norm_and_send(g, carry):
         norm_group(g)
@@ -297,7 +297,7 @@
                 emit(1, b, s, whole(b, s, fx, fy), half_2)
             return carry
 
-        lax.fori_loop(0, GS, lambda t, k: one(g * GS + t, k), 0, unroll=3)
+        lax.fori_loop(0, GS, lambda t, k: one(g * GS + t, k), 0, unroll=6)
         for c in copies(1, g):
             c.start()
         return carry
@@ -358,11 +358,11 @@
                 came[parts * s + j][p] = rows[j * CR : (j + 1) * CR]
             return carry
 
-        lax.fori_loop(6, S, sent, 0, unroll=3)
+        lax.fori_loop(6, S, sent, 0, unroll=6)
         for c in range(parts * s, parts * (s + 1)):
             for d in range(1, 4):
                 y_copy(c, d).start()
-        lax.fori_loop(0, 6, kept, 0, unroll=3)
+        lax.fori_loop(0, 6, kept, 0, unroll=6)
 
     run_inner(1, (1, 2))
     wait_faces(1, slice(0, 2))
@@ -435,22 +435,22 @@
             ready[c][p] = came[c][picks[p]]
             return carry
 
-        lax.fori_loop(0, S, gather, 0, unroll=4)
+        lax.fori_loop(0, S, gather, 0, unroll=8)
         for d in range(1, 4):
             z_copy(c, d).start()
         own_copy(c).start()
 
     order = [parts * s + j for s in (1, 2, 0, 3) for j in range(parts)]
-    run_inner(1, (0, 3))
-    for c in order[:1]:
-        relay(c)
+    run_inner(1, (0,))
+    relay(order[0])
+    run_inner(1, (3,))
+    relay(order[1])
     wait_faces(1, slice(2, 4))
     lax.fori_loop(0, S, y_one, 0, unroll=8)
     hidden(0)
-    for c in order[1:2]:
-        relay(c)
+    relay(order[2])
     hidden(3)
-    for c in order[2:]:
+    for c in order[3:]:
         relay(c)
 
     def finish(g, carry):

time: 91.8 us -> 90.6 us (0.987)
  Pallas kernels: 89.1 us -> 87.9 us
    pallas_call x1, Pallas kernels: 75.2 us -> 74.1 us  [main(): pl.pallas_call(main_kernel, out_shape=(jax.ShapeDtypeStruct((S, CELLS, C)...]
where the time goes in v4:
time: 90.6 us; the launch traced here: 90.4 us
  Pallas kernels  87.9 us (97%)
  local copies, waits for them, and re-layouts  2.54 us (3%)
    pallas_call x1, Pallas kernels, main(): pl.pallas_call(main_kernel, out_shape=(jax.ShapeDtypeStruct((S, CELLS, C)...  74.1 us
    pallas_call x1, Pallas kernels, raise_(): pl.pallas_call(raise_kernel, out_shape=jax.ShapeDtypeStruct((8 * S, CELLS...  13.8 us

profile of v4, /device:TPU:1, one launch (start us, length us, event | category | flops | bytes accessed | tf_op | source)
XLA Modules:
  0.0 90.4 jit_solution(4192985838363957685)
XLA Ops:
  0.0 0.7 copy.15
  0.7 0.6 reshape.31.owner
  1.3 0.7 copy.14
  2.0 0.6 reshape.33.slot
  2.5 74.1 %main.1 = (bf16[24,512,128]{2,1,0:T(8,128)(2,1)}, s32[24]{0:T(128)}) custom-call(bf16[24,512,128]{2,1,0:T(8,128)(2,1)} %bitcast.17, f32[1,128]{1,0:T(1,128)} %bitcast.18, bf16[7,128,128]{2,1,0:T(8,128)(2,1)} %k1_hbm.1, f32[1,128]{1,0:T(1,128)} %bitcast.19, bf16[7,128,128]{2,1,0:T(8,128)(2,1)} %k2_hbm.1, s32[6,1,24]{2,1,0:T(1,128)} %reshape.31.owner, ...), custom_call_target="tpu_custom_call" | custom-call | flops 7000000000 | bytes 8000000 | tf_op jit(solution)/shard_map/main/pallas_call | solution.py:477
  76.6 13.8 %raise.1 = bf16[192,512,128]{2,1,0:T(8,128)(2,1)} custom-call(s32[24]{0:T(128)} %get-tuple-element.7.index, bf16[24,512,128]{2,1,0:T(8,128)(2,1)} %get-tuple-element.8.moved, bf16[2,2,2,128,128]{4,3,2,1,0:T(8,128)(2,1)} %up.1), custom_call_target="tpu_custom_call" | custom-call | tf_op jit(solution)/shard_map/raise/pallas_call | solution.py:587
